TPU v7x, 512 devices: a whole 4x8x8 slice. The times are simulated.
512 devices in a mesh: row: 32 (over z, x), col: 16 (over y, core).
Axes of the slice: x: 4, y: 8, z: 8, core: 2. Of those that a mesh axis runs over, the one named last changes fastest.
Arguments:
- inputs: bfloat16 [768, 12288], P('row', 'col'), may hold values from -6 to 6
- weight: bfloat16 [12288, 49152], P('col', 'row'), may hold values from -0.0546875 to 0.0546875
- cotangent: bfloat16 [768, 49152], P('col', 'row'), may hold values from -6 to 6
Outputs:
- activated: bfloat16 [768, 49152], P('col', 'row')
- grad_inputs: bfloat16 [768, 12288], P('row', 'col')
- grad_weight: bfloat16 [12288, 49152], P('col', 'row')
All inputs are finite; a program needn't handle non-finite values.
Results may differ from a plain program's by a relative error of at most 0.025.
Values may be sent and summed in bfloat16 or wider, within the bound.
No kernel may reach another device: no remote copies, remote signals or barrier semaphores. Data moves between devices by JAX's collectives and lax.ppermute only.
A program may use at most 64 MiB of HBM per device.

v0:
```python
import jax
import jax.numpy as jnp
from jax import lax
from jax.sharding import PartitionSpec as P


def gelu_parts(preact):
    tanh_arg = 0.7978845608 * (preact + 0.044715 * preact * preact * preact)
    tanh_value = jnp.tanh(tanh_arg)
    activated = 0.5 * preact * (1.0 + tanh_value)
    slopes = 0.5 * (1.0 + tanh_value) + 0.5 * preact * (
        1.0 - tanh_value * tanh_value
    ) * 0.7978845608 * (1.0 + 3.0 * 0.044715 * preact * preact)
    return (activated, slopes)


def body(inputs, weight, cotangent):
    gathered = lax.all_gather(inputs, "row", axis=0, tiled=True)
    tile_rows = gathered
    preact = lax.psum_scatter(
        jnp.dot(tile_rows, weight, preferred_element_type=jnp.float32).astype(jnp.bfloat16),
        "col",
        scatter_dimension=0,
        tiled=True,
    ).astype(jnp.float32)
    gelu_local, slopes = gelu_parts(preact)
    activated = gelu_local.astype(jnp.bfloat16)
    local_grad = (cotangent.astype(jnp.float32) * slopes).astype(jnp.bfloat16)
    hidden_grad = lax.all_gather(local_grad, "col", axis=0, tiled=True)
    tile_rows = hidden_grad
    grad_inputs = lax.psum_scatter(
        lax.dot_general(
            tile_rows, weight, (((1,), (1,)), ((), ())), preferred_element_type=jnp.float32
        ).astype(jnp.bfloat16),
        "row",
        scatter_dimension=0,
        tiled=True,
    )
    grad_weight = lax.dot_general(
        gathered, hidden_grad, (((0,), (0,)), ((), ())), preferred_element_type=jnp.float32
    ).astype(jnp.bfloat16)
    return (activated, grad_inputs, grad_weight)


def solution(mesh):
    return jax.shard_map(
        body,
        mesh=mesh,
        in_specs=(P("row", "col"), P("col", "row"), P("col", "row")),
        out_specs=(P("col", "row"), P("row", "col"), P("col", "row")),
        check_vma=False,
    )
```

profile of v0, /device:TPU:8, one launch (start us, length us, event | category | flops | bytes accessed | tf_op | source)
XLA Modules:
  0.0 425.7 jit_solution(5881928390002292388)
XLA Ops:
  7.2 0.0 copy-start
  7.2 0.0 all-gather.3.cloned.1.call-start
  7.2 0.7 all-gather.3.cloned.1.call-update
  7.9 0.0 reduce-scatter.3.cloned.1.call-start
  8.0 90.5 %all-gather.3.cloned.1.call-done = bf16[768,768]{1,0:T(8,128)(2,1)} async-done(((bf16[24,768]{1,0:T(8,128)(2,1)}), bf16[768,768]{1,0:T(8,128)(2,1)}) %all-gather.3.cloned.1.call-update) | async-done | bytes 1179664 | tf_op jit(solution)/shard_map/all_gather | solution.py:18
  98.4 0.0 copy-done
  98.4 4.7 %convolution_convert_fusion.1 = bf16[768,1536]{1,0:T(8,128)(2,1)} fusion(bf16[768,768]{1,0:T(8,128)(2,1)} %all-gather.3.cloned.1.call-done, bf16[768,1536]{1,0:T(8,128)(2,1)S(1)} %copy-done), kind=kOutput, calls=%fused_computation.1 | convolution fusion | flops 1813118976 | bytes 5898240 | tf_op jit(solution)/shard_map/dot_general | solution.py:21
  103.1 0.0 copy-start.1
  103.1 0.0 reduce-scatter.3.cloned.1.call-update
  103.1 0.0 all-gather.5.cloned.1.call-start
  103.2 56.4 %reduce-scatter.3.cloned.1.call-done = bf16[48,1536]{1,0:T(8,128)(2,1)} async-done(((bf16[768,1536]{1,0:T(8,128)(2,1)}), bf16[48,1536]{1,0:T(8,128)(2,1)}) %reduce-scatter.3.cloned.1.call-update) | async-done | bytes 147472 | tf_op jit(solution)/shard_map/reduce_scatter | solution.py:20
  159.6 0.0 copy-done.1
  159.6 1.8 fusion.8
  161.4 0.0 all-gather.5.cloned.1.call-update
  161.5 0.0 copy-start.2
  161.5 0.0 reduce-scatter.5.cloned.1.call-start
  161.5 45.0 %all-gather.5.cloned.1.call-done = bf16[768,1536]{1,0:T(8,128)(2,1)} async-done(((bf16[48,1536]{1,0:T(8,128)(2,1)}), bf16[768,1536]{1,0:T(8,128)(2,1)}) %all-gather.5.cloned.1.call-update) | async-done | bytes 2359312 | tf_op jit(solution)/shard_map/all_gather | solution.py:29
  206.5 4.8 %convolution_convert_fusion.2 = bf16[768,768]{1,0:T(8,128)(2,1)} fusion(bf16[768,1536]{1,0:T(8,128)(2,1)} %all-gather.5.cloned.1.call-done, bf16[768,1536]{1,0:T(8,128)(2,1)S(1)} %copy-done), kind=kOutput, calls=%fused_computation.3 | convolution fusion | flops 1812529152 | bytes 5898240 | tf_op jit(solution)/shard_map/dot_general | solution.py:32
  211.3 0.0 reduce-scatter.5.cloned.1.call-update
  211.3 0.0 copy-done.2
  211.3 5.1 %fusion = bf16[768,1536]{0,1:T(8,128)(2,1)} fusion(bf16[768,1536]{1,0:T(8,128)(2,1)} %all-gather.5.cloned.1.call-done, bf16[768,768]{1,0:T(8,128)(2,1)S(1)} %copy-done.2), kind=kOutput, calls=%fused_computation.2 | convolution fusion | flops 1813118976 | bytes 5898240 | tf_op jit(solution)/shard_map/dot_general | solution.py:39
  216.4 4.3 %copy.6 = bf16[768,1536]{1,0:T(8,128)(2,1)} copy(bf16[768,1536]{0,1:T(8,128)(2,1)} %fusion) | data formatting | bytes 4718592
  220.7 198.5 %reduce-scatter.5.cloned.1.call-done = bf16[24,768]{1,0:T(8,128)(2,1)} async-done(((bf16[768,768]{1,0:T(8,128)(2,1)}), bf16[24,768]{1,0:T(8,128)(2,1)}) %reduce-scatter.5.cloned.1.call-update) | async-done | bytes 36880 | tf_op jit(solution)/shard_map/reduce_scatter | solution.py:31
Async XLA Ops:
  7.2 91.3 %copy-start = (bf16[768,1536]{1,0:T(8,128)(2,1)S(1)}, bf16[768,1536]{1,0:T(8,128)(2,1)}, u32[]{:S(2)}) copy-start(bf16[768,1536]{1,0:T(8,128)(2,1)} %param.4) | copy-start | bytes 7077892
  7.2 91.2 %all-gather.3.cloned.1.call-start = ((), (), s32[]{:S(2)}) async-start(), calls=%async_computation.2 | async-start | bytes 1216512 | tf_op jit(solution)/shard_map/all_gather | solution.py:18
  7.9 151.7 %reduce-scatter.3.cloned.1.call-start = ((), (), s32[]{:S(2)}) async-start(), calls=%async_computation.3 | async-start | bytes 2506752 | tf_op jit(solution)/shard_map/reduce_scatter | solution.py:20
  103.1 56.5 %copy-start.1 = (bf16[48,1536]{1,0:T(8,128)(2,1)S(1)}, bf16[48,1536]{1,0:T(8,128)(2,1)}, u32[]{:S(2)}) copy-start(bf16[48,1536]{1,0:T(8,128)(2,1)} %param.5) | copy-start | bytes 442372
  103.1 103.4 %all-gather.5.cloned.1.call-start = ((), (), s32[]{:S(2)}) async-start(), calls=%async_computation.4 | async-start | bytes 2506752 | tf_op jit(solution)/shard_map/all_gather | solution.py:29
  161.5 49.8 %copy-start.2 = (bf16[768,768]{1,0:T(8,128)(2,1)S(1)}, bf16[768,768]{1,0:T(8,128)(2,1)}, u32[]{:S(2)}) copy-start(bf16[768,768]{1,0:T(8,128)(2,1)} %all-gather.3.cloned.1.call-done) | copy-start | bytes 3538948
  161.5 257.7 %reduce-scatter.5.cloned.1.call-start = ((), (), s32[]{:S(2)}) async-start(), calls=%async_computation.5 | async-start | bytes 1216512 | tf_op jit(solution)/shard_map/reduce_scatter | solution.py:31
Sparse Core Ops, SparseCore 0:
  11.2 87.1 all-gather.2
  103.2 56.3 reduce-scatter.2
  162.3 44.1 all-gather.4
  211.4 207.7 reduce-scatter.4
where the time goes:
time: 426 us
  waiting for transfers between devices  391 us (92%)
  matrix products  14.5 us (3%)
  between operations  13.8 us (3%)
  local copies, waits for them, and re-layouts  4.28 us (1%)
    reduce_scatter x1, waiting for transfers between devices, body(): lax.psum_scatter(lax.dot_general(tile_rows, weight, (((1,), (1,)), ((), (...  199 us
    all_gather x1, waiting for transfers between devices, body(): gathered = lax.all_gather(inputs, 'row', axis=0, tiled=True)  90.5 us
    reduce_scatter x1, waiting for transfers between devices, body(): lax.psum_scatter(jnp.dot(tile_rows, weight, preferred_element_type=jnp.fl...  56.4 us
    all_gather x1, waiting for transfers between devices, body(): hidden_grad = lax.all_gather(local_grad, 'col', axis=0, tiled=True)  45 us
  transfers between devices with their start and end apart: 4, of which 4 were waited for; matrix products, arithmetic and copies ran while one was open for 2% of the time, Pallas kernels for 0%

commit v1 on v0

v1 whole, which is shorter than its diff:
```python
import jax
import jax.numpy as jnp
from jax import lax
from jax.sharding import Mesh
from jax.sharding import PartitionSpec as P

Z, X, Y, C = 8, 4, 8, 2


def gelu_parts(preact):
    tanh_arg = 0.7978845608 * (preact + 0.044715 * preact * preact * preact)
    tanh_value = jnp.tanh(tanh_arg)
    activated = 0.5 * preact * (1.0 + tanh_value)
    slopes = 0.5 * (1.0 + tanh_value) + 0.5 * preact * (
        1.0 - tanh_value * tanh_value
    ) * 0.7978845608 * (1.0 + 3.0 * 0.044715 * preact * preact)
    return (activated, slopes)


def exchange(x, axis):
    return lax.all_to_all(x, axis, 0, 0, tiled=True)


def spread(x, axis, n):
    return exchange(jnp.broadcast_to(x[None], (n, *x.shape)), axis)


def swap_cores(x):
    return lax.ppermute(x, "c", [(0, 1), (1, 0)])


def total(x):
    return jnp.sum(x.astype(jnp.float32), axis=0)


def body(inputs, weight, cotangent):
    core = lax.axis_index("c")
    tokens, width = inputs.shape
    rows, hidden = cotangent.shape

    by_z = spread(inputs, "z", Z)
    by_x = spread(by_z.reshape(Z * tokens, width), "x", X)
    gathered = by_x.reshape(X, Z, tokens, width).transpose(1, 0, 2, 3).reshape(-1, width)

    partial = jnp.dot(gathered, weight, preferred_element_type=jnp.float32)
    partial = partial.astype(jnp.bfloat16).reshape(Y, C, rows, hidden)
    mine = lax.dynamic_index_in_dim(partial, core, 1, keepdims=False)
    theirs = lax.dynamic_index_in_dim(partial, 1 - core, 1, keepdims=False)
    pair = (mine.astype(jnp.float32) + swap_cores(theirs).astype(jnp.float32)).astype(jnp.bfloat16)
    preact = total(exchange(pair, "y"))

    gelu_local, slopes = gelu_parts(preact)
    activated = gelu_local.astype(jnp.bfloat16)
    local_grad = (cotangent.astype(jnp.float32) * slopes).astype(jnp.bfloat16)

    mine = spread(local_grad, "y", Y)
    theirs = swap_cores(mine)
    first = jnp.where(core == 0, mine, theirs)
    second = jnp.where(core == 0, theirs, mine)
    hidden_grad = jnp.stack([first, second], axis=1).reshape(-1, hidden)

    partial = lax.dot_general(
        hidden_grad, weight, (((1,), (1,)), ((), ())), preferred_element_type=jnp.float32
    ).astype(jnp.bfloat16)
    partial = partial.reshape(Z, X, tokens, width).transpose(1, 0, 2, 3)
    sums = total(exchange(partial, "x")).astype(jnp.bfloat16)
    grad_inputs = total(exchange(sums, "z")).astype(jnp.bfloat16)

    grad_weight = lax.dot_general(
        gathered, hidden_grad, (((0,), (0,)), ((), ())), preferred_element_type=jnp.float32
    ).astype(jnp.bfloat16)
    return (activated, grad_inputs, grad_weight)


def solution(mesh):
    grid = Mesh(mesh.devices.reshape(Z, X, Y, C), ("z", "x", "y", "c"))
    row, col = ("z", "x"), ("y", "c")
    return jax.shard_map(
        body,
        mesh=grid,
        in_specs=(P(row, col), P(col, row), P(col, row)),
        out_specs=(P(col, row), P(row, col), P(col, row)),
        check_vma=False,
    )
```

time: 426 us -> 173 us (0.41)
  waiting for transfers between devices: 391 us -> 22.9 us
  blocking collectives: 0 us -> 113 us
  between operations: 13.8 us -> 0.78 us
  starting transfers between devices: 0.16 us -> 11.6 us
  matrix products: 14.5 us -> 9.45 us
  local copies, waits for them, and re-layouts: 4.28 us -> 8.73 us
  other arithmetic: 1.84 us -> 6.19 us
    reduce_scatter x2 -> x0, waiting for transfers between devices: 255 us -> none  [the longest x1 199 us: body(): lax.psum_scatter(lax.dot_general(tile_rows, weight, (((1,), (1,)), ((), (...]
    all_gather x2 -> x0, waiting for transfers between devices: 135 us -> none  [the longest x1 90.5 us: body(): gathered = lax.all_gather(inputs, 'row', axis=0, tiled=True)]
    all_to_all x0 -> x4, blocking collectives: none -> 113 us  [exchange(): return lax.all_to_all(x, axis, 0, 0, tiled=True)]
    all_to_all x0 -> x2, waiting for transfers between devices: none -> 17 us  [exchange(): return lax.all_to_all(x, axis, 0, 0, tiled=True)]
    all_to_all x0 -> x2, starting transfers between devices: none -> 7.74 us  [exchange(): return lax.all_to_all(x, axis, 0, 0, tiled=True)]
    ppermute x0 -> x2, waiting for transfers between devices: none -> 5.88 us  [swap_cores(): return lax.ppermute(x, 'c', [(0, 1), (1, 0)])]
    dot_general x2, matrix products: 9.42 us -> 4.01 us  [the longest x1 2.02 us: body(): lax.dot_general(hidden_grad, weight, (((1,), (1,)), ((), ())), preferred_...]
  transfers between devices with their start and end apart: 4 -> 4, of which waited for: 4 -> 4; matrix products, arithmetic and copies ran while one was open for 2% -> 6% of each run, Pallas kernels for 0% -> 0%
where the time goes in v1:
time: 173 us
  blocking collectives  113 us (65%)
  waiting for transfers between devices  22.9 us (13%)
  starting transfers between devices  11.6 us (7%)
  matrix products  9.45 us (5%)
  local copies, waits for them, and re-layouts  8.73 us (5%)
  other arithmetic  6.19 us (4%)
    all_to_all x4, blocking collectives, exchange(): return lax.all_to_all(x, axis, 0, 0, tiled=True)  113 us
    all_to_all x2, waiting for transfers between devices, exchange(): return lax.all_to_all(x, axis, 0, 0, tiled=True)  17 us
    all_to_all x2, starting transfers between devices, exchange(): return lax.all_to_all(x, axis, 0, 0, tiled=True)  7.74 us
    unnamed x11, local copies, waits for them, and re-layouts  6.33 us
    ppermute x2, waiting for transfers between devices, swap_cores(): return lax.ppermute(x, 'c', [(0, 1), (1, 0)])  5.88 us
    dot_general x1, matrix products, body(): lax.dot_general(gathered, hidden_grad, (((0,), (0,)), ((), ())), preferre...  5.44 us
    ppermute x2, starting transfers between devices, swap_cores(): return lax.ppermute(x, 'c', [(0, 1), (1, 0)])  3.82 us
  transfers between devices with their start and end apart: 4, of which 4 were waited for; matrix products, arithmetic and copies ran while one was open for 6% of the time, Pallas kernels for 0%

profile of v1, /device:TPU:8, one launch (start us, length us, event | category | flops | bytes accessed | tf_op | source)
XLA Modules:
  0.0 172.6 jit_solution(7931933710530239064)
XLA Ops:
  0.6 0.9 broadcast_in_dim.8
  1.6 22.7 %all_to_all.30 = bf16[8,24,768]{2,1,0:T(8,128)(2,1)S(1)} all-to-all(bf16[8,24,768]{2,1,0:T(8,128)(2,1)S(1)} %broadcast_in_dim.8), channel_id=1, replica_groups=mesh['z'=8,'x'=4,'y'=8,'c'=2] {'z'}, dimensions={0} | all-to-all | bytes 589824 | tf_op jit(solution)/shard_map/all_to_all | solution.py:21
  24.3 1.1 broadcast_in_dim.10
  25.4 4.3 %all-to-all-start.1 = ((bf16[4,192,768]{2,1,0:T(8,128)(2,1)}), bf16[4,192,768]{2,1,0:T(8,128)(2,1)S(1)}, u32[]{:S(2)}, u32[]{:S(2)}) async-start(bf16[4,192,768]{2,1,0:T(8,128)(2,1)} %broadcast_in_dim.10), calls=%async_computation.1 | async-start | bytes 2359296 | tf_op jit(solution)/shard_map/all_to_all | solution.py:21
  29.7 14.5 %all-to-all-done.1 = bf16[4,192,768]{2,1,0:T(8,128)(2,1)S(1)} async-done(((bf16[4,192,768]{2,1,0:T(8,128)(2,1)}), bf16[4,192,768]{2,1,0:T(8,128)(2,1)S(1)}, u32[]{:S(2)}, u32[]{:S(2)}) %all-to-all-start.1) | async-done | bytes 1179680 | tf_op jit(solution)/shard_map/all_to_all | solution.py:21
  44.3 2.0 %convolution_convert_fusion.1 = bf16[768,1536]{1,0:T(8,128)(2,1)S(1)} fusion(bf16[768,768]{1,0:T(8,128)(2,1)S(1)} %bitcast.36, bf16[768,1536]{1,0:T(8,128)(2,1)S(1)} %copy-done), kind=kOutput, calls=%fused_computation.1 | convolution fusion | flops 1813118976 | bytes 5898240 | tf_op jit(solution)/shard_map/dot_general | solution.py:45
  46.4 1.3 copy-done.1
  47.7 1.9 %collective-permute-start = (bf16[8,48,1536]{2,1,0:T(8,128)(2,1)S(1)}, bf16[8,48,1536]{2,1,0:T(8,128)(2,1)}, u32[]{:S(2)}, u32[]{:S(2)}) collective-permute-start(bf16[8,48,1536]{2,1,0:T(8,128)(2,1)S(1)} %dynamic-slice_bitcast_fusion), channel_id=1, source_target_pairs={{0,1},{1,0},{2,3},{3,2},{4,5},{5,4},{6,7},{7,6},{8,9},{9,8},{10,11... | collective-permute-start | bytes 3538952 | tf_op jit(solution)/shard_map/ppermute | solution.py:29
  49.6 2.9 %collective-permute-done = bf16[8,48,1536]{2,1,0:T(8,128)(2,1)} collective-permute-done((bf16[8,48,1536]{2,1,0:T(8,128)(2,1)S(1)}, bf16[8,48,1536]{2,1,0:T(8,128)(2,1)}, u32[]{:S(2)}, u32[]{:S(2)}) %collective-permute-start) | collective-permute-done | bytes 1179680 | tf_op jit(solution)/shard_map/ppermute | solution.py:29
  52.5 1.9 %fusion.1 = bf16[8,48,1536]{2,1,0:T(8,128)(2,1)S(1)} fusion(bf16[8,48,1536]{2,1,0:T(8,128)(2,1)} %collective-permute-done, bf16[8,2,48,1536]{3,2,1,0:T(8,128)(2,1)} %bitcast.33, s32[]{:T(128)S(6)} %select_n.19), kind=kLoop, calls=%fused_computation.5 | loop fusion | flops 2359296 | bytes 3538948 | tf_op jit(solution)/shard_map/convert_element_type | solution.py:49
  54.5 37.7 %all_to_all.31 = bf16[8,48,1536]{2,1,0:T(8,128)(2,1)S(1)} all-to-all(bf16[8,48,1536]{2,1,0:T(8,128)(2,1)S(1)} %fusion.1), channel_id=1, replica_groups=mesh['z'=8,'x'=4,'y'=8,'c'=2] {'y'}, dimensions={0} | all-to-all | bytes 2359296 | tf_op jit(solution)/shard_map/all_to_all | solution.py:21
  92.3 0.8 copy-done.4
  93.1 0.9 fusion.8
  94.1 33.1 %all_to_all.32 = bf16[8,48,1536]{2,1,0:T(8,128)(2,1)S(1)} all-to-all(bf16[8,48,1536]{2,1,0:T(8,128)(2,1)S(1)} %broadcast_in_dim.22), channel_id=1, replica_groups=mesh['z'=8,'x'=4,'y'=8,'c'=2] {'y'}, dimensions={0} | all-to-all | bytes 2359296 | tf_op jit(solution)/shard_map/all_to_all | solution.py:21
  127.2 1.9 %collective-permute-start.1 = (bf16[8,48,1536]{2,1,0:T(8,128)(2,1)S(1)}, bf16[8,48,1536]{2,1,0:T(8,128)(2,1)}, u32[]{:S(2)}, u32[]{:S(2)}) collective-permute-start(bf16[8,48,1536]{2,1,0:T(8,128)(2,1)S(1)} %all_to_all.32), channel_id=1, source_target_pairs={{0,1},{1,0},{2,3},{3,2},{4,5},{5,4},{6,7},{7,6},{8,9},{9,8},{10,11... | collective-permute-start | bytes 3538952 | tf_op jit(solution)/shard_map/ppermute | solution.py:29
  129.1 2.9 %collective-permute-done.1 = bf16[8,48,1536]{2,1,0:T(8,128)(2,1)} collective-permute-done((bf16[8,48,1536]{2,1,0:T(8,128)(2,1)S(1)}, bf16[8,48,1536]{2,1,0:T(8,128)(2,1)}, u32[]{:S(2)}, u32[]{:S(2)}) %collective-permute-start.1) | collective-permute-done | bytes 1179680 | tf_op jit(solution)/shard_map/ppermute | solution.py:29
  132.1 1.4 select_bitcast_fusion.1
  133.7 2.0 %convolution_convert_fusion.2 = bf16[768,768]{1,0:T(8,128)(2,1)S(1)} fusion(bf16[768,1536]{1,0:T(8,128)(2,1)S(1)} %bitcast.34, bf16[768,1536]{1,0:T(8,128)(2,1)S(1)} %copy-done), kind=kOutput, calls=%fused_computation.7 | convolution fusion | flops 1812529152 | bytes 5898240 | tf_op jit(solution)/shard_map/dot_general | solution.py:62
  135.9 19.5 %all_to_all.33 = bf16[4,8,24,768]{3,2,1,0:T(8,128)(2,1)S(1)} all-to-all(bf16[4,8,24,768]{3,2,1,0:T(8,128)(2,1)S(1)} %bitcast.31), channel_id=1, replica_groups=mesh['z'=8,'x'=4,'y'=8,'c'=2] {'x'}, dimensions={0} | all-to-all | bytes 2359296 | tf_op jit(solution)/shard_map/all_to_all | solution.py:21
  155.4 0.9 reduce_sum.34
  156.3 3.4 %all-to-all-start.5 = ((bf16[8,24,768]{2,1,0:T(8,128)(2,1)}), bf16[8,24,768]{2,1,0:T(8,128)(2,1)S(1)}, u32[]{:S(2)}, u32[]{:S(2)}) async-start(bf16[8,24,768]{2,1,0:T(8,128)(2,1)} %reduce_sum.34), calls=%async_computation.5 | async-start | bytes 589824 | tf_op jit(solution)/shard_map/all_to_all | solution.py:21
  159.8 5.4 %fusion = bf16[768,1536]{0,1:T(8,128)(2,1)} fusion(bf16[768,1536]{1,0:T(8,128)(2,1)} %bitcast.35, bf16[768,768]{1,0:T(8,128)(2,1)} %bitcast.37), kind=kOutput, calls=%fused_computation.2 | convolution fusion | flops 1813118976 | bytes 5898240 | tf_op jit(solution)/shard_map/dot_general | solution.py:69
  165.2 4.3 %copy.19 = bf16[768,1536]{1,0:T(8,128)(2,1)} copy(bf16[768,1536]{0,1:T(8,128)(2,1)} %fusion) | data formatting | bytes 4718592
  169.5 2.5 %all-to-all-done.5 = bf16[8,24,768]{2,1,0:T(8,128)(2,1)S(1)} async-done(((bf16[8,24,768]{2,1,0:T(8,128)(2,1)}), bf16[8,24,768]{2,1,0:T(8,128)(2,1)S(1)}, u32[]{:S(2)}, u32[]{:S(2)}) %all-to-all-start.5) | async-done | bytes 294944 | tf_op jit(solution)/shard_map/all_to_all | solution.py:21
  (15 shorter events, 1.4 us)
Async XLA Ops:
  0.6 43.6 %copy-start = (bf16[768,1536]{1,0:T(8,128)(2,1)S(1)}, bf16[768,1536]{1,0:T(8,128)(2,1)}, u32[]{:S(2)}) copy-start(bf16[768,1536]{1,0:T(8,128)(2,1)} %param.4) | copy-start | bytes 7077892
  25.4 18.8 %all-to-all-start.1 = ((bf16[4,192,768]{2,1,0:T(8,128)(2,1)}), bf16[4,192,768]{2,1,0:T(8,128)(2,1)S(1)}, u32[]{:S(2)}, u32[]{:S(2)}) async-start(bf16[4,192,768]{2,1,0:T(8,128)(2,1)} %broadcast_in_dim.10), calls=%async_computation.1 | async-start | bytes 2359296 | tf_op jit(solution)/shard_map/all_to_all | solution.py:21
  44.2 2.0 %copy-start.3 = (bf16[8,4,24,768]{3,2,1,0:T(8,128)(2,1)}, bf16[8,4,24,768]{3,2,1,0:T(8,128)(2,1)S(1)}, u32[]{:S(2)}) copy-start(bf16[8,4,24,768]{3,2,1,0:T(8,128)(2,1)S(1)} %copy.16) | copy-start | bytes 3538948
  46.3 1.4 copy-start.1
  47.7 4.9 %collective-permute-start = (bf16[8,48,1536]{2,1,0:T(8,128)(2,1)S(1)}, bf16[8,48,1536]{2,1,0:T(8,128)(2,1)}, u32[]{:S(2)}, u32[]{:S(2)}) collective-permute-start(bf16[8,48,1536]{2,1,0:T(8,128)(2,1)S(1)} %dynamic-slice_bitcast_fusion), channel_id=1, source_target_pairs={{0,1},{1,0},{2,3},{3,2},{4,5},{5,4},{6,7},{7,6},{8,9},{9,8},{10,11... | collective-permute-start | bytes 3538952 | tf_op jit(solution)/shard_map/ppermute | solution.py:29
  92.2 0.9 copy-start.4
  127.2 4.9 %collective-permute-start.1 = (bf16[8,48,1536]{2,1,0:T(8,128)(2,1)S(1)}, bf16[8,48,1536]{2,1,0:T(8,128)(2,1)}, u32[]{:S(2)}, u32[]{:S(2)}) collective-permute-start(bf16[8,48,1536]{2,1,0:T(8,128)(2,1)S(1)} %all_to_all.32), channel_id=1, source_target_pairs={{0,1},{1,0},{2,3},{3,2},{4,5},{5,4},{6,7},{7,6},{8,9},{9,8},{10,11... | collective-permute-start | bytes 3538952 | tf_op jit(solution)/shard_map/ppermute | solution.py:29
  133.7 2.0 %copy-start.2 = (bf16[8,2,48,1536]{3,2,1,0:T(8,128)(2,1)}, bf16[8,2,48,1536]{3,2,1,0:T(8,128)(2,1)S(1)}, u32[]{:S(2)}) copy-start(bf16[8,2,48,1536]{3,2,1,0:T(8,128)(2,1)S(1)} %pad_maximum_fusion) | copy-start | bytes 7077892
  156.3 15.7 %all-to-all-start.5 = ((bf16[8,24,768]{2,1,0:T(8,128)(2,1)}), bf16[8,24,768]{2,1,0:T(8,128)(2,1)S(1)}, u32[]{:S(2)}, u32[]{:S(2)}) async-start(bf16[8,24,768]{2,1,0:T(8,128)(2,1)} %reduce_sum.34), calls=%async_computation.5 | async-start | bytes 589824 | tf_op jit(solution)/shard_map/all_to_all | solution.py:21

commit v2 on v1

v2 whole, which is shorter than its diff:
```python
import jax
import jax.numpy as jnp
from jax import lax
from jax.sharding import Mesh
from jax.sharding import PartitionSpec as P

Z, X, Y, C = 8, 4, 8, 2
ALL = ("z", "x", "y", "c")


def gelu_parts(preact):
    tanh_arg = 0.7978845608 * (preact + 0.044715 * preact * preact * preact)
    tanh_value = jnp.tanh(tanh_arg)
    activated = 0.5 * preact * (1.0 + tanh_value)
    slopes = 0.5 * (1.0 + tanh_value) + 0.5 * preact * (
        1.0 - tanh_value * tanh_value
    ) * 0.7978845608 * (1.0 + 3.0 * 0.044715 * preact * preact)
    return (activated, slopes)


def z_groups():
    groups = []
    for x in range(X):
        for y in range(Y):
            for c in range(C):
                sign = 1 if c == 0 else -1
                groups.append([(((y + sign * j) % Z * X + x) * Y + y) * C + c for j in range(Z)])
    return groups


def exchange_z(x):
    return lax.all_to_all(x, ALL, 0, 0, tiled=True, axis_index_groups=z_groups())


def exchange_x(x):
    return lax.all_to_all(x, "x", 0, 0, tiled=True)


def copies(x, n):
    return jnp.broadcast_to(x[None], (n, *x.shape))


def swap_cores(x):
    return lax.ppermute(x, "c", [(0, 1), (1, 0)])


def send(x, distance):
    pairs = []
    for y in range(Y):
        pairs.append((y * C, (y + distance) % Y * C))
        pairs.append((y * C + 1, (y - distance) % Y * C + 1))
    return lax.ppermute(x, ("y", "c"), pairs)


def f32(x):
    return x.astype(jnp.float32)


def bf16(x):
    return x.astype(jnp.bfloat16)


def total(x):
    return jnp.sum(f32(x), axis=0)


def body(inputs, weight, cotangent):
    core = lax.axis_index("c")
    first = core == 0
    tokens, width = inputs.shape
    rows, hidden = cotangent.shape
    half = hidden // 2
    block = X * tokens

    def half_of(x):
        return jnp.where(first, x[:, :half], x[:, half:])

    other = swap_cores(cotangent)
    cotangents = jnp.concatenate(
        [jnp.where(first, cotangent, other), jnp.where(first, other, cotangent)], axis=0
    )

    by_z = exchange_z(copies(inputs, Z))
    by_x = exchange_x(copies(by_z, X).reshape(X, Z, tokens, width))
    gathered = by_x.transpose(1, 0, 2, 3).reshape(Z, block, width)

    def product(lo, hi):
        out = jnp.dot(
            gathered[lo:hi].reshape(-1, width), weight, preferred_element_type=jnp.float32
        )
        return bf16(out).reshape(hi - lo, block, hidden)

    far = product(4, 6)
    far_other = swap_cores(far)
    near = product(6, 8)
    near_other = swap_cores(near)
    mine = product(0, 4)

    four = bf16(half_of(f32(far[0]) + f32(far_other[0])))
    three = bf16(f32(mine[3]) + f32(far_other[1]))
    four = send(four, 2)
    three = send(three, 1)
    one = send(bf16(f32(mine[1]) + f32(near_other[1])), 1)
    two = f32(mine[2]) + f32(near_other[0]) + f32(three)
    zero = jnp.zeros_like(four)
    four = jnp.concatenate(
        [jnp.where(first, four, zero), jnp.where(first, zero, four)], axis=1
    )
    two = send(bf16(two + f32(four)), 2)
    partial = f32(mine[0]) + f32(one) + f32(two)
    preact = partial + f32(swap_cores(bf16(partial)))

    gelu_local, slopes = gelu_parts(preact)
    activated = bf16(jnp.where(first, gelu_local[:rows], gelu_local[rows:]))
    own = bf16(f32(cotangents) * slopes)

    two = send(own, 2)
    one = send(own, 1)
    three = send(two, 1)
    four = send(half_of(two), 2)
    four_other = swap_cores(four)
    four = jnp.concatenate(
        [jnp.where(first, four, four_other), jnp.where(first, four_other, four)], axis=1
    )
    hidden_grad = jnp.concatenate(
        [own, swap_cores(one), swap_cores(two), swap_cores(three), four, three, two, one], axis=0
    )

    partial = bf16(
        lax.dot_general(
            hidden_grad, weight, (((1,), (1,)), ((), ())), preferred_element_type=jnp.float32
        )
    )
    partial = partial.reshape(Z, X, tokens, width).transpose(1, 0, 2, 3)
    sums = bf16(total(exchange_x(partial)))
    grad_inputs = bf16(total(exchange_z(sums)))

    grad_weight = bf16(
        lax.dot_general(
            gathered.reshape(-1, width),
            hidden_grad,
            (((0,), (0,)), ((), ())),
            preferred_element_type=jnp.float32,
        )
    )
    return (activated, grad_inputs, grad_weight)


def solution(mesh):
    grid = Mesh(mesh.devices.reshape(Z, X, Y, C), ALL)
    row, col = ("z", "x"), ("y", "c")
    return jax.shard_map(
        body,
        mesh=grid,
        in_specs=(P(row, col), P(col, row), P(col, row)),
        out_specs=(P(col, row), P(row, col), P(col, row)),
        check_vma=False,
    )
```

time: 173 us -> 170 us (0.983)
  blocking collectives: 113 us -> 43.2 us
  starting transfers between devices: 11.6 us -> 56.1 us
  waiting for transfers between devices: 22.9 us -> 43.5 us
    all_to_all x4 -> x2, blocking collectives: 113 us -> 43.2 us  [the longest x1 22.7 us: exchange_z(): lax.all_to_all(x, ALL, 0, 0, tiled=True, axis_index_groups=z_groups())]
    ppermute x0 -> x8, starting transfers between devices: none -> 27.1 us  [send(): return lax.ppermute(x, ('y', 'c'), pairs)]
    ppermute x0 -> x8, waiting for transfers between devices: none -> 26.2 us  [send(): return lax.ppermute(x, ('y', 'c'), pairs)]
    ppermute x2 -> x8, starting transfers between devices: 3.82 us -> 16.5 us  [swap_cores(): return lax.ppermute(x, 'c', [(0, 1), (1, 0)])]
    all_to_all x2, starting transfers between devices: 7.74 us -> 12.5 us  [the longest x1 8.24 us: exchange_z(): lax.all_to_all(x, ALL, 0, 0, tiled=True, axis_index_groups=z_groups())]
    ppermute x2 -> x8, waiting for transfers between devices: 5.88 us -> 2.58 us  [swap_cores(): return lax.ppermute(x, 'c', [(0, 1), (1, 0)])]
    all_to_all x2, waiting for transfers between devices: 17 us -> 14.8 us  [the longest x1 14.8 us: exchange_x(): return lax.all_to_all(x, 'x', 0, 0, tiled=True)]
    reduce_sum x3 -> x2, other arithmetic: 1.75 us -> 3.87 us  [total(): return jnp.sum(f32(x), axis=0)]
  transfers between devices with their start and end apart: 4 -> 18, of which waited for: 4 -> 10; matrix products, arithmetic and copies ran while one was open for 6% -> 8% of each run, Pallas kernels for 0% -> 0%
where the time goes in v2:
time: 170 us; the launch traced here: 169 us
  starting transfers between devices  56.1 us (33%)
  waiting for transfers between devices  43.5 us (26%)
  blocking collectives  43.2 us (25%)
  matrix products  9.5 us (6%)
  local copies, waits for them, and re-layouts  7.97 us (5%)
  other arithmetic  7.4 us (4%)
    ppermute x8, starting transfers between devices, send(): return lax.ppermute(x, ('y', 'c'), pairs)  27.1 us
    ppermute x8, waiting for transfers between devices, send(): return lax.ppermute(x, ('y', 'c'), pairs)  26.2 us
    all_to_all x1, blocking collectives, exchange_z(): lax.all_to_all(x, ALL, 0, 0, tiled=True, axis_index_groups=z_groups())  22.7 us
    all_to_all x1, blocking collectives, exchange_x(): return lax.all_to_all(x, 'x', 0, 0, tiled=True)  20.5 us
    ppermute x8, starting transfers between devices, swap_cores(): return lax.ppermute(x, 'c', [(0, 1), (1, 0)])  16.5 us
    all_to_all x1, waiting for transfers between devices, exchange_x(): return lax.all_to_all(x, 'x', 0, 0, tiled=True)  14.8 us
    all_to_all x1, starting transfers between devices, exchange_z(): lax.all_to_all(x, ALL, 0, 0, tiled=True, axis_index_groups=z_groups())  8.24 us
    dot_general x1, matrix products, body(): lax.dot_general(gathered.reshape(-1, width), hidden_grad, (((0,), (0,)),...  5.15 us
  transfers between devices with their start and end apart: 18, of which 10 were waited for; matrix products, arithmetic and copies ran while one was open for 8% of the time, Pallas kernels for 0%

profile of v2, /device:TPU:8, one launch (start us, length us, event | category | flops | bytes accessed | tf_op | source)
XLA Modules:
  0.0 168.7 jit_solution(3881500205581239939)
XLA Ops:
  1.6 22.7 %all_to_all.20 = bf16[8,24,768]{2,1,0:T(8,128)(2,1)S(1)} all-to-all(bf16[8,24,768]{2,1,0:T(8,128)(2,1)S(1)} %broadcast_in_dim.6), channel_id=1, replica_groups={{0,64,128,192,256,320,384,448},{1,449,385,321,257,193,129,65},{66,130,1..., dimensions={0} | all-to-all | bytes 589824 | tf_op jit(solution)/shard_map/all_to_all | solution.py:32
  25.4 4.3 %all-to-all-start.1 = ((bf16[4,8,24,768]{3,2,1,0:T(8,128)(2,1)}), bf16[4,8,24,768]{3,2,1,0:T(8,128)(2,1)}, u32[]{:S(2)}, u32[]{:S(2)}) async-start(bf16[4,8,24,768]{3,2,1,0:T(8,128)(2,1)} %broadcast_in_dim.7), calls=%async_computation.1 | async-start | bytes 2359296 | tf_op jit(solution)/shard_map/all_to_all | solution.py:36
  29.7 14.8 %all-to-all-done.1 = bf16[4,8,24,768]{3,2,1,0:T(8,128)(2,1)} async-done(((bf16[4,8,24,768]{3,2,1,0:T(8,128)(2,1)}), bf16[4,8,24,768]{3,2,1,0:T(8,128)(2,1)}, u32[]{:S(2)}, u32[]{:S(2)}) %all-to-all-start.1) | async-done | bytes 1179680 | tf_op jit(solution)/shard_map/all_to_all | solution.py:36
  49.1 2.4 %collective-permute-start = (bf16[2,96,1536]{2,1,0:T(8,128)(2,1)S(1)}, bf16[2,96,1536]{2,1,0:T(8,128)(2,1)S(1)}, u32[]{:S(2)}, u32[]{:S(2)}) collective-permute-start(bf16[2,96,1536]{2,1,0:T(8,128)(2,1)S(1)} %bitcast.53), channel_id=1, source_target_pairs={{0,1},{1,0},{2,3},{3,2},{4,5},{5,4},{6,7},{7,6},{8,9},{9,8},{10,11... | collective-permute-start | bytes 1769480 | tf_op jit(solution)/shard_map/ppermute | solution.py:44
  52.8 6.2 %collective-permute-start.4 = (bf16[96,768]{1,0:T(8,128)(2,1)S(1)}, bf16[96,768]{1,0:T(8,128)(2,1)S(1)}, u32[]{:S(2)}, u32[]{:S(2)}) collective-permute-start(bf16[96,768]{1,0:T(8,128)(2,1)S(1)} %fusion.14), channel_id=1, source_target_pairs={{0,4},{1,13},{2,6},{3,15},{4,8},{5,1},{6,10},{7,3},{8,12},{9,5},{1... | collective-permute-start | bytes 442376 | tf_op jit(solution)/shard_map/ppermute | solution.py:52
  59.0 2.7 %collective-permute-start.3 = (bf16[96,1536]{1,0:T(8,128)(2,1)S(1)}, bf16[96,1536]{1,0:T(8,128)(2,1)S(1)}, u32[]{:S(2)}, u32[]{:S(2)}) collective-permute-start(bf16[96,1536]{1,0:T(8,128)(2,1)S(1)} %fusion.8), channel_id=1, source_target_pairs={{0,2},{1,15},{2,4},{3,1},{4,6},{5,3},{6,8},{7,5},{8,10},{9,7},{10,... | collective-permute-start | bytes 884744 | tf_op jit(solution)/shard_map/ppermute | solution.py:52
  63.5 4.1 %collective-permute-done.3 = bf16[96,1536]{1,0:T(8,128)(2,1)S(1)} collective-permute-done((bf16[96,1536]{1,0:T(8,128)(2,1)S(1)}, bf16[96,1536]{1,0:T(8,128)(2,1)S(1)}, u32[]{:S(2)}, u32[]{:S(2)}) %collective-permute-start.3) | collective-permute-done | bytes 294944 | tf_op jit(solution)/shard_map/ppermute | solution.py:52
  67.9 3.3 %collective-permute-start.5 = (bf16[96,1536]{1,0:T(8,128)(2,1)S(1)}, bf16[96,1536]{1,0:T(8,128)(2,1)S(1)}, u32[]{:S(2)}, u32[]{:S(2)}) collective-permute-start(bf16[96,1536]{1,0:T(8,128)(2,1)S(1)} %get-tuple-element.19), channel_id=1, source_target_pairs={{0,4},{1,13},{2,6},{3,15},{4,8},{5,1},{6,10},{7,3},{8,12},{9,5},{1... | collective-permute-start | bytes 884744 | tf_op jit(solution)/shard_map/ppermute | solution.py:52
  71.2 3.8 %collective-permute-start.1 = (bf16[96,1536]{1,0:T(8,128)(2,1)S(1)}, bf16[96,1536]{1,0:T(8,128)(2,1)S(1)}, u32[]{:S(2)}, u32[]{:S(2)}) collective-permute-start(bf16[96,1536]{1,0:T(8,128)(2,1)S(1)} %get-tuple-element.18), channel_id=1, source_target_pairs={{0,2},{1,15},{2,4},{3,1},{4,6},{5,3},{6,8},{7,5},{8,10},{9,7},{10,... | collective-permute-start | bytes 884744 | tf_op jit(solution)/shard_map/ppermute | solution.py:52
  76.9 4.9 %collective-permute-done.5 = bf16[96,1536]{1,0:T(8,128)(2,1)S(1)} collective-permute-done((bf16[96,1536]{1,0:T(8,128)(2,1)S(1)}, bf16[96,1536]{1,0:T(8,128)(2,1)S(1)}, u32[]{:S(2)}, u32[]{:S(2)}) %collective-permute-start.5) | collective-permute-done | bytes 294944 | tf_op jit(solution)/shard_map/ppermute | solution.py:52
  87.9 3.1 %collective-permute-start.8 = (bf16[96,1536]{1,0:T(8,128)(2,1)S(1)}, bf16[96,1536]{1,0:T(8,128)(2,1)S(1)}, u32[]{:S(2)}, u32[]{:S(2)}) collective-permute-start(bf16[96,1536]{1,0:T(8,128)(2,1)S(1)} %get-tuple-element.16), channel_id=1, source_target_pairs={{0,2},{1,15},{2,4},{3,1},{4,6},{5,3},{6,8},{7,5},{8,10},{9,7},{10,... | collective-permute-start | bytes 884744 | tf_op jit(solution)/shard_map/ppermute | solution.py:52
  91.0 4.2 %collective-permute-start.10 = (bf16[96,1536]{1,0:T(8,128)(2,1)S(1)}, bf16[96,1536]{1,0:T(8,128)(2,1)S(1)}, u32[]{:S(2)}, u32[]{:S(2)}) collective-permute-start(bf16[96,1536]{1,0:T(8,128)(2,1)S(1)} %get-tuple-element.16), channel_id=1, source_target_pairs={{0,4},{1,13},{2,6},{3,15},{4,8},{5,1},{6,10},{7,3},{8,12},{9,5},{1... | collective-permute-start | bytes 884744 | tf_op jit(solution)/shard_map/ppermute | solution.py:52
  96.9 1.9 %collective-permute-start.9 = (bf16[96,1536]{1,0:T(8,128)(2,1)S(1)}, bf16[96,1536]{1,0:T(8,128)(2,1)S(1)}, u32[]{:S(2)}, u32[]{:S(2)}) collective-permute-start(bf16[96,1536]{1,0:T(8,128)(2,1)S(1)} %collective-permute-done.8), channel_id=1, source_target_pairs={{0,1},{1,0},{2,3},{3,2},{4,5},{5,4},{6,7},{7,6},{8,9},{9,8},{10,11... | collective-permute-start | bytes 884744 | tf_op jit(solution)/shard_map/ppermute | solution.py:44
  98.9 7.0 %collective-permute-done.10 = bf16[96,1536]{1,0:T(8,128)(2,1)S(1)} collective-permute-done((bf16[96,1536]{1,0:T(8,128)(2,1)S(1)}, bf16[96,1536]{1,0:T(8,128)(2,1)S(1)}, u32[]{:S(2)}, u32[]{:S(2)}) %collective-permute-start.10) | collective-permute-done | bytes 294944 | tf_op jit(solution)/shard_map/ppermute | solution.py:52
  107.8 2.0 %collective-permute-start.14 = (bf16[96,768]{1,0:T(8,128)(2,1)S(1)}, bf16[96,768]{1,0:T(8,128)(2,1)S(1)}, u32[]{:S(2)}, u32[]{:S(2)}) collective-permute-start(bf16[96,768]{1,0:T(8,128)(2,1)S(1)} %slice_select_fusion.2), channel_id=1, source_target_pairs={{0,4},{1,13},{2,6},{3,15},{4,8},{5,1},{6,10},{7,3},{8,12},{9,5},{1... | collective-permute-start | bytes 442376 | tf_op jit(solution)/shard_map/ppermute | solution.py:52
  109.8 2.1 %collective-permute-start.11 = (bf16[96,1536]{1,0:T(8,128)(2,1)S(1)}, bf16[96,1536]{1,0:T(8,128)(2,1)S(1)}, u32[]{:S(2)}, u32[]{:S(2)}) collective-permute-start(bf16[96,1536]{1,0:T(8,128)(2,1)S(1)} %collective-permute-done.10), channel_id=1, source_target_pairs={{0,1},{1,0},{2,3},{3,2},{4,5},{5,4},{6,7},{7,6},{8,9},{9,8},{10,11... | collective-permute-start | bytes 884744 | tf_op jit(solution)/shard_map/ppermute | solution.py:44
  111.9 5.4 %collective-permute-done.14 = bf16[96,768]{1,0:T(8,128)(2,1)S(1)} collective-permute-done((bf16[96,768]{1,0:T(8,128)(2,1)S(1)}, bf16[96,768]{1,0:T(8,128)(2,1)S(1)}, u32[]{:S(2)}, u32[]{:S(2)}) %collective-permute-start.14) | collective-permute-done | bytes 147488 | tf_op jit(solution)/shard_map/ppermute | solution.py:52
  119.2 2.4 %collective-permute-start.13 = (bf16[96,1536]{1,0:T(8,128)(2,1)S(1)}, bf16[96,1536]{1,0:T(8,128)(2,1)S(1)}, u32[]{:S(2)}, u32[]{:S(2)}) collective-permute-start(bf16[96,1536]{1,0:T(8,128)(2,1)S(1)} %collective-permute-done.12), channel_id=1, source_target_pairs={{0,1},{1,0},{2,3},{3,2},{4,5},{5,4},{6,7},{7,6},{8,9},{9,8},{10,11... | collective-permute-start | bytes 884744 | tf_op jit(solution)/shard_map/ppermute | solution.py:44
  123.0 2.0 %convolution_convert_fusion.4 = bf16[768,768]{1,0:T(8,128)(2,1)S(1)} fusion(bf16[768,1536]{1,0:T(8,128)(2,1)S(1)} %constant_dynamic-update-slice_fusion, bf16[768,1536]{1,0:T(8,128)(2,1)S(1)} %copy-done), kind=kOutput, calls=%fused_computation.5 | convolution fusion | flops 1812529152 | bytes 5898240 | tf_op jit(solution)/shard_map/dot_general | solution.py:130
  125.1 20.5 %all_to_all.21 = bf16[4,8,24,768]{3,2,1,0:T(8,128)(2,1)} all-to-all(bf16[4,8,24,768]{3,2,1,0:T(8,128)(2,1)S(1)} %bitcast.48), channel_id=1, replica_groups=mesh['z'=8,'x'=4,'y'=8,'c'=2] {'x'}, dimensions={0} | all-to-all | bytes 2359296 | tf_op jit(solution)/shard_map/all_to_all | solution.py:36
  145.5 2.2 %reduce_sum.24 = bf16[8,24,768]{2,1,0:T(8,128)(2,1)} reduce(bf16[4,8,24,768]{3,2,1,0:T(8,128)(2,1)} %all_to_all.21, bf16[]{:T(256)} %constant.3.clone.1), dimensions={0}, to_apply=%region_0.1 | reduce | flops 442368 | bytes 1474562 | tf_op jit(solution)/shard_map/reduce_sum | solution.py:64
  147.8 8.2 %all-to-all-start.3 = ((bf16[8,24,768]{2,1,0:T(8,128)(2,1)}), bf16[8,24,768]{2,1,0:T(8,128)(2,1)}, u32[]{:S(2)}, u32[]{:S(2)}) async-start(bf16[8,24,768]{2,1,0:T(8,128)(2,1)} %reduce_sum.24), calls=%async_computation.3 | async-start | bytes 589824 | tf_op jit(solution)/shard_map/all_to_all | solution.py:32
  157.7 5.1 %fusion = bf16[768,1536]{0,1:T(8,128)(2,1)} fusion(bf16[768,1536]{1,0:T(8,128)(2,1)} %copy-done.2, bf16[768,768]{1,0:T(8,128)(2,1)S(1)} %bitcast.47), kind=kOutput, calls=%fused_computation.1 | convolution fusion | flops 1813118976 | bytes 5898240 | tf_op jit(solution)/shard_map/dot_general | solution.py:139
  162.8 4.3 %copy.13 = bf16[768,1536]{1,0:T(8,128)(2,1)} copy(bf16[768,1536]{0,1:T(8,128)(2,1)} %fusion) | data formatting | bytes 4718592
  (52 shorter events, 28.0 us)
Async XLA Ops:
  0.6 45.3 %copy-start = (bf16[768,1536]{1,0:T(8,128)(2,1)S(1)}, bf16[768,1536]{1,0:T(8,128)(2,1)}, u32[]{:S(2)}) copy-start(bf16[768,1536]{1,0:T(8,128)(2,1)} %param.4) | copy-start | bytes 7077892
  25.4 19.1 %all-to-all-start.1 = ((bf16[4,8,24,768]{3,2,1,0:T(8,128)(2,1)}), bf16[4,8,24,768]{3,2,1,0:T(8,128)(2,1)}, u32[]{:S(2)}, u32[]{:S(2)}) async-start(bf16[4,8,24,768]{3,2,1,0:T(8,128)(2,1)} %broadcast_in_dim.7), calls=%async_computation.1 | async-start | bytes 2359296 | tf_op jit(solution)/shard_map/all_to_all | solution.py:36
  46.6 6.1 %collective-permute-start.2 = (bf16[2,96,1536]{2,1,0:T(8,128)(2,1)S(1)}, bf16[2,96,1536]{2,1,0:T(8,128)(2,1)S(1)}, u32[]{:S(2)}, u32[]{:S(2)}) collective-permute-start(bf16[2,96,1536]{2,1,0:T(8,128)(2,1)S(1)} %bitcast.49), channel_id=1, source_target_pairs={{0,1},{1,0},{2,3},{3,2},{4,5},{5,4},{6,7},{7,6},{8,9},{9,8},{10,11... | collective-permute-start | bytes 1769480 | tf_op jit(solution)/shard_map/ppermute | solution.py:44
  49.1 14.4 %collective-permute-start = (bf16[2,96,1536]{2,1,0:T(8,128)(2,1)S(1)}, bf16[2,96,1536]{2,1,0:T(8,128)(2,1)S(1)}, u32[]{:S(2)}, u32[]{:S(2)}) collective-permute-start(bf16[2,96,1536]{2,1,0:T(8,128)(2,1)S(1)} %bitcast.53), channel_id=1, source_target_pairs={{0,1},{1,0},{2,3},{3,2},{4,5},{5,4},{6,7},{7,6},{8,9},{9,8},{10,11... | collective-permute-start | bytes 1769480 | tf_op jit(solution)/shard_map/ppermute | solution.py:44
  52.6 22.4 %copy-start.1 = (bf16[48,1536]{1,0:T(8,128)(2,1)S(1)}, bf16[48,1536]{1,0:T(8,128)(2,1)}, u32[]{:S(2)}) copy-start(bf16[48,1536]{1,0:T(8,128)(2,1)} %param.5) | copy-start | bytes 442372
  52.8 10.7 %collective-permute-start.4 = (bf16[96,768]{1,0:T(8,128)(2,1)S(1)}, bf16[96,768]{1,0:T(8,128)(2,1)S(1)}, u32[]{:S(2)}, u32[]{:S(2)}) collective-permute-start(bf16[96,768]{1,0:T(8,128)(2,1)S(1)} %fusion.14), channel_id=1, source_target_pairs={{0,4},{1,13},{2,6},{3,15},{4,8},{5,1},{6,10},{7,3},{8,12},{9,5},{1... | collective-permute-start | bytes 442376 | tf_op jit(solution)/shard_map/ppermute | solution.py:52
  59.0 8.6 %collective-permute-start.3 = (bf16[96,1536]{1,0:T(8,128)(2,1)S(1)}, bf16[96,1536]{1,0:T(8,128)(2,1)S(1)}, u32[]{:S(2)}, u32[]{:S(2)}) collective-permute-start(bf16[96,1536]{1,0:T(8,128)(2,1)S(1)} %fusion.8), channel_id=1, source_target_pairs={{0,2},{1,15},{2,4},{3,1},{4,6},{5,3},{6,8},{7,5},{8,10},{9,7},{10,... | collective-permute-start | bytes 884744 | tf_op jit(solution)/shard_map/ppermute | solution.py:52
  67.9 14.0 %collective-permute-start.5 = (bf16[96,1536]{1,0:T(8,128)(2,1)S(1)}, bf16[96,1536]{1,0:T(8,128)(2,1)S(1)}, u32[]{:S(2)}, u32[]{:S(2)}) collective-permute-start(bf16[96,1536]{1,0:T(8,128)(2,1)S(1)} %get-tuple-element.19), channel_id=1, source_target_pairs={{0,4},{1,13},{2,6},{3,15},{4,8},{5,1},{6,10},{7,3},{8,12},{9,5},{1... | collective-permute-start | bytes 884744 | tf_op jit(solution)/shard_map/ppermute | solution.py:52
  71.2 11.9 %collective-permute-start.1 = (bf16[96,1536]{1,0:T(8,128)(2,1)S(1)}, bf16[96,1536]{1,0:T(8,128)(2,1)S(1)}, u32[]{:S(2)}, u32[]{:S(2)}) collective-permute-start(bf16[96,1536]{1,0:T(8,128)(2,1)S(1)} %get-tuple-element.18), channel_id=1, source_target_pairs={{0,2},{1,15},{2,4},{3,1},{4,6},{5,3},{6,8},{7,5},{8,10},{9,7},{10,... | collective-permute-start | bytes 884744 | tf_op jit(solution)/shard_map/ppermute | solution.py:52
  75.0 10.1 %collective-permute-start.7 = (bf16[48,1536]{1,0:T(8,128)(2,1)S(1)}, bf16[48,1536]{1,0:T(8,128)(2,1)S(1)}, u32[]{:S(2)}, u32[]{:S(2)}) collective-permute-start(bf16[48,1536]{1,0:T(8,128)(2,1)S(1)} %copy-done.1), channel_id=1, source_target_pairs={{0,1},{1,0},{2,3},{3,2},{4,5},{5,4},{6,7},{7,6},{8,9},{9,8},{10,11... | collective-permute-start | bytes 442376 | tf_op jit(solution)/shard_map/ppermute | solution.py:44
  83.2 3.5 %collective-permute-start.6 = (bf16[96,1536]{1,0:T(8,128)(2,1)S(1)}, bf16[96,1536]{1,0:T(8,128)(2,1)S(1)}, u32[]{:S(2)}, u32[]{:S(2)}) collective-permute-start(bf16[96,1536]{1,0:T(8,128)(2,1)S(1)} %fusion.15), channel_id=1, source_target_pairs={{0,1},{1,0},{2,3},{3,2},{4,5},{5,4},{6,7},{7,6},{8,9},{9,8},{10,11... | collective-permute-start | bytes 884744 | tf_op jit(solution)/shard_map/ppermute | solution.py:44
  87.9 9.0 %collective-permute-start.8 = (bf16[96,1536]{1,0:T(8,128)(2,1)S(1)}, bf16[96,1536]{1,0:T(8,128)(2,1)S(1)}, u32[]{:S(2)}, u32[]{:S(2)}) collective-permute-start(bf16[96,1536]{1,0:T(8,128)(2,1)S(1)} %get-tuple-element.16), channel_id=1, source_target_pairs={{0,2},{1,15},{2,4},{3,1},{4,6},{5,3},{6,8},{7,5},{8,10},{9,7},{10,... | collective-permute-start | bytes 884744 | tf_op jit(solution)/shard_map/ppermute | solution.py:52
  91.0 14.9 %collective-permute-start.10 = (bf16[96,1536]{1,0:T(8,128)(2,1)S(1)}, bf16[96,1536]{1,0:T(8,128)(2,1)S(1)}, u32[]{:S(2)}, u32[]{:S(2)}) collective-permute-start(bf16[96,1536]{1,0:T(8,128)(2,1)S(1)} %get-tuple-element.16), channel_id=1, source_target_pairs={{0,4},{1,13},{2,6},{3,15},{4,8},{5,1},{6,10},{7,3},{8,12},{9,5},{1... | collective-permute-start | bytes 884744 | tf_op jit(solution)/shard_map/ppermute | solution.py:52
  96.9 24.7 %collective-permute-start.9 = (bf16[96,1536]{1,0:T(8,128)(2,1)S(1)}, bf16[96,1536]{1,0:T(8,128)(2,1)S(1)}, u32[]{:S(2)}, u32[]{:S(2)}) collective-permute-start(bf16[96,1536]{1,0:T(8,128)(2,1)S(1)} %collective-permute-done.8), channel_id=1, source_target_pairs={{0,1},{1,0},{2,3},{3,2},{4,5},{5,4},{6,7},{7,6},{8,9},{9,8},{10,11... | collective-permute-start | bytes 884744 | tf_op jit(solution)/shard_map/ppermute | solution.py:44
  105.9 13.3 %collective-permute-start.12 = (bf16[96,1536]{1,0:T(8,128)(2,1)S(1)}, bf16[96,1536]{1,0:T(8,128)(2,1)S(1)}, u32[]{:S(2)}, u32[]{:S(2)}) collective-permute-start(bf16[96,1536]{1,0:T(8,128)(2,1)S(1)} %collective-permute-done.10), channel_id=1, source_target_pairs={{0,2},{1,15},{2,4},{3,1},{4,6},{5,3},{6,8},{7,5},{8,10},{9,7},{10,... | collective-permute-start | bytes 884744 | tf_op jit(solution)/shard_map/ppermute | solution.py:52
  107.8 9.4 %collective-permute-start.14 = (bf16[96,768]{1,0:T(8,128)(2,1)S(1)}, bf16[96,768]{1,0:T(8,128)(2,1)S(1)}, u32[]{:S(2)}, u32[]{:S(2)}) collective-permute-start(bf16[96,768]{1,0:T(8,128)(2,1)S(1)} %slice_select_fusion.2), channel_id=1, source_target_pairs={{0,4},{1,13},{2,6},{3,15},{4,8},{5,1},{6,10},{7,3},{8,12},{9,5},{1... | collective-permute-start | bytes 442376 | tf_op jit(solution)/shard_map/ppermute | solution.py:52
  109.8 11.8 %collective-permute-start.11 = (bf16[96,1536]{1,0:T(8,128)(2,1)S(1)}, bf16[96,1536]{1,0:T(8,128)(2,1)S(1)}, u32[]{:S(2)}, u32[]{:S(2)}) collective-permute-start(bf16[96,1536]{1,0:T(8,128)(2,1)S(1)} %collective-permute-done.10), channel_id=1, source_target_pairs={{0,1},{1,0},{2,3},{3,2},{4,5},{5,4},{6,7},{7,6},{8,9},{9,8},{10,11... | collective-permute-start | bytes 884744 | tf_op jit(solution)/shard_map/ppermute | solution.py:44
  117.3 4.4 %collective-permute-start.15 = (bf16[96,768]{1,0:T(8,128)(2,1)S(1)}, bf16[96,768]{1,0:T(8,128)(2,1)S(1)}, u32[]{:S(2)}, u32[]{:S(2)}) collective-permute-start(bf16[96,768]{1,0:T(8,128)(2,1)S(1)} %collective-permute-done.14), channel_id=1, source_target_pairs={{0,1},{1,0},{2,3},{3,2},{4,5},{5,4},{6,7},{7,6},{8,9},{9,8},{10,11... | collective-permute-start | bytes 442376 | tf_op jit(solution)/shard_map/ppermute | solution.py:44
  119.2 3.6 %collective-permute-start.13 = (bf16[96,1536]{1,0:T(8,128)(2,1)S(1)}, bf16[96,1536]{1,0:T(8,128)(2,1)S(1)}, u32[]{:S(2)}, u32[]{:S(2)}) collective-permute-start(bf16[96,1536]{1,0:T(8,128)(2,1)S(1)} %collective-permute-done.12), channel_id=1, source_target_pairs={{0,1},{1,0},{2,3},{3,2},{4,5},{5,4},{6,7},{7,6},{8,9},{9,8},{10,11... | collective-permute-start | bytes 884744 | tf_op jit(solution)/shard_map/ppermute | solution.py:44
  122.9 2.0 %copy-start.2 = (bf16[768,1536]{1,0:T(8,128)(2,1)}, bf16[768,1536]{1,0:T(8,128)(2,1)S(1)}, u32[]{:S(2)}) copy-start(bf16[768,1536]{1,0:T(8,128)(2,1)S(1)} %constant_dynamic-update-slice_fusion) | copy-start | bytes 7077892
  147.8 19.3 %all-to-all-start.3 = ((bf16[8,24,768]{2,1,0:T(8,128)(2,1)}), bf16[8,24,768]{2,1,0:T(8,128)(2,1)}, u32[]{:S(2)}, u32[]{:S(2)}) async-start(bf16[8,24,768]{2,1,0:T(8,128)(2,1)} %reduce_sum.24), calls=%async_computation.3 | async-start | bytes 589824 | tf_op jit(solution)/shard_map/all_to_all | solution.py:32

commit v3 on v2

--- a/solution.py
+++ b/solution.py
@@ -1,6 +1,8 @@
 import jax
 import jax.numpy as jnp
 from jax import lax
+from jax.experimental import pallas as pl
+from jax.experimental.pallas import tpu as pltpu
 from jax.sharding import Mesh
 from jax.sharding import PartitionSpec as P
 
@@ -64,6 +66,31 @@
     return jnp.sum(f32(x), axis=0)
 
 
+def outer(x, y, columns=256):
+    def kernel(x_ref, y_ref, out_ref):
+        out_ref[...] = lax.dot_general(
+            x_ref[...], y_ref[...], (((0,), (0,)), ((), ())), preferred_element_type=jnp.float32
+        ).astype(out_ref.dtype)
+
+    (rows, left), right = x.shape, y.shape[1]
+    return pl.pallas_call(
+        kernel,
+        grid=(right // columns,),
+        in_specs=[
+            pl.BlockSpec((rows, left), lambda i: (0, 0)),
+            pl.BlockSpec((rows, columns), lambda i: (0, i)),
+        ],
+        out_specs=pl.BlockSpec((left, columns), lambda i: (0, i)),
+        out_shape=jax.ShapeDtypeStruct((left, right), x.dtype),
+        compiler_params=pltpu.CompilerParams(vmem_limit_bytes=16 * 2**20),
+        cost_estimate=pl.CostEstimate(
+            flops=2 * rows * left * right,
+            bytes_accessed=2 * (rows * left + rows * right + left * right),
+            transcendentals=0,
+        ),
+    )(x, y)
+
+
 def body(inputs, weight, cotangent):
     core = lax.axis_index("c")
     first = core == 0
@@ -82,26 +109,21 @@
 
     by_z = exchange_z(copies(inputs, Z))
     by_x = exchange_x(copies(by_z, X).reshape(X, Z, tokens, width))
+    by_x, cotangents = lax.optimization_barrier((by_x, cotangents))
     gathered = by_x.transpose(1, 0, 2, 3).reshape(Z, block, width)
 
-    def product(lo, hi):
-        out = jnp.dot(
-            gathered[lo:hi].reshape(-1, width), weight, preferred_element_type=jnp.float32
-        )
-        return bf16(out).reshape(hi - lo, block, hidden)
+    def product(x):
+        out = jnp.dot(x.reshape(-1, width), weight, preferred_element_type=jnp.float32)
+        return bf16(out).reshape(-1, block, hidden)
 
-    far = product(4, 6)
-    far_other = swap_cores(far)
-    near = product(6, 8)
-    near_other = swap_cores(near)
-    mine = product(0, 4)
-
-    four = bf16(half_of(f32(far[0]) + f32(far_other[0])))
-    three = bf16(f32(mine[3]) + f32(far_other[1]))
-    four = send(four, 2)
-    three = send(three, 1)
-    one = send(bf16(f32(mine[1]) + f32(near_other[1])), 1)
-    two = f32(mine[2]) + f32(near_other[0]) + f32(three)
+    lent = product(gathered[4:8])
+    theirs = swap_cores(lent)
+    mine = product(gathered[0:4])
+    four = send(bf16(half_of(f32(lent[0]) + f32(theirs[0]))), 2)
+    ahead = [bf16(f32(mine[3]) + f32(theirs[1])), bf16(f32(mine[1]) + f32(theirs[3]))]
+    ahead = send(jnp.concatenate(ahead, axis=0), 1)
+    three, one = ahead[:block], ahead[block:]
+    two = f32(mine[2]) + f32(theirs[2]) + f32(three)
     zero = jnp.zeros_like(four)
     four = jnp.concatenate(
         [jnp.where(first, four, zero), jnp.where(first, zero, four)], axis=1
@@ -117,13 +139,19 @@
     two = send(own, 2)
     one = send(own, 1)
     three = send(two, 1)
-    four = send(half_of(two), 2)
-    four_other = swap_cores(four)
+    four = half_of(two)
+    early, four, activated = lax.optimization_barrier(
+        (jnp.concatenate([one, two], axis=0), four, activated)
+    )
+    four = send(four, 2)
+    early = swap_cores(early)
+    late = swap_cores(jnp.concatenate([three, four], axis=1))
+    four_other = late[:, hidden:]
     four = jnp.concatenate(
         [jnp.where(first, four, four_other), jnp.where(first, four_other, four)], axis=1
     )
     hidden_grad = jnp.concatenate(
-        [own, swap_cores(one), swap_cores(two), swap_cores(three), four, three, two, one], axis=0
+        [own, early, late[:, :hidden], four, three, two, one], axis=0
     )
 
     partial = bf16(
@@ -132,17 +160,9 @@
         )
     )
     partial = partial.reshape(Z, X, tokens, width).transpose(1, 0, 2, 3)
+    grad_weight = outer(gathered.reshape(-1, width), hidden_grad)
     sums = bf16(total(exchange_x(partial)))
     grad_inputs = bf16(total(exchange_z(sums)))
-
-    grad_weight = bf16(
-        lax.dot_general(
-            gathered.reshape(-1, width),
-            hidden_grad,
-            (((0,), (0,)), ((), ())),
-            preferred_element_type=jnp.float32,
-        )
-    )
     return (activated, grad_inputs, grad_weight)
 
 

time: 170 us -> 162 us (0.953)
  matrix products: 9.5 us -> 4.18 us
  Pallas kernels: 0 us -> 4.45 us
  starting transfers between devices: 56.1 us -> 53.4 us
  local copies, waits for them, and re-layouts: 7.97 us -> 5.38 us
    ppermute x8 -> x5, starting transfers between devices: 16.5 us -> 9.6 us  [swap_cores(): return lax.ppermute(x, 'c', [(0, 1), (1, 0)])]
    dot_general x4 -> x2, matrix products: 7.47 us -> 2.15 us  [product(): jnp.dot(x.reshape(-1, width), weight, preferred_element_type=jnp.float32)]
    all_to_all x1, waiting for transfers between devices: 0.01 us -> 4.71 us  [exchange_z(): lax.all_to_all(x, ALL, 0, 0, tiled=True, axis_index_groups=z_groups())]
    ppermute x8 -> x7, waiting for transfers between devices: 26.2 us -> 21.5 us  [send(): return lax.ppermute(x, ('y', 'c'), pairs)]
    ppermute x8 -> x7, starting transfers between devices: 27.1 us -> 31.7 us  [send(): return lax.ppermute(x, ('y', 'c'), pairs)]
    pallas_call x0 -> x1, Pallas kernels: none -> 4.45 us  [outer(): pl.pallas_call(kernel, grid=(right // columns,), in_specs=[pl.BlockSpec((...]
    all_to_all x1, waiting for transfers between devices: 14.8 us -> 10.8 us  [exchange_x(): return lax.all_to_all(x, 'x', 0, 0, tiled=True)]
    ppermute x8 -> x5, waiting for transfers between devices: 2.58 us -> 6.31 us  [swap_cores(): return lax.ppermute(x, 'c', [(0, 1), (1, 0)])]
  transfers between devices with their start and end apart: 18 -> 14, of which waited for: 10 -> 11; matrix products, arithmetic and copies ran while one was open for 8% -> 2% of each run, Pallas kernels for 0% -> 3%
where the time goes in v3:
time: 162 us; the launch traced here: 161 us
  starting transfers between devices  53.4 us (33%)
  waiting for transfers between devices  43.3 us (27%)
  blocking collectives  42.9 us (26%)
  other arithmetic  6.56 us (4%)
  local copies, waits for them, and re-layouts  5.38 us (3%)
  Pallas kernels  4.45 us (3%)
  matrix products  4.18 us (3%)
    ppermute x7, starting transfers between devices, send(): return lax.ppermute(x, ('y', 'c'), pairs)  31.7 us
    all_to_all x1, blocking collectives, exchange_z(): lax.all_to_all(x, ALL, 0, 0, tiled=True, axis_index_groups=z_groups())  22.7 us
    ppermute x7, waiting for transfers between devices, send(): return lax.ppermute(x, ('y', 'c'), pairs)  21.5 us
    all_to_all x1, blocking collectives, exchange_x(): return lax.all_to_all(x, 'x', 0, 0, tiled=True)  20.2 us
    all_to_all x1, waiting for transfers between devices, exchange_x(): return lax.all_to_all(x, 'x', 0, 0, tiled=True)  10.8 us
    ppermute x5, starting transfers between devices, swap_cores(): return lax.ppermute(x, 'c', [(0, 1), (1, 0)])  9.6 us
    all_to_all x1, starting transfers between devices, exchange_z(): lax.all_to_all(x, ALL, 0, 0, tiled=True, axis_index_groups=z_groups())  7.81 us
    ppermute x5, waiting for transfers between devices, swap_cores(): return lax.ppermute(x, 'c', [(0, 1), (1, 0)])  6.31 us
  transfers between devices with their start and end apart: 14, of which 11 were waited for; matrix products, arithmetic and copies ran while one was open for 2% of the time, Pallas kernels for 3%

profile of v3, /device:TPU:8, one launch (start us, length us, event | category | flops | bytes accessed | tf_op | source)
XLA Modules:
  0.0 161.1 jit_solution(12189672915440955089)
XLA Ops:
  1.6 22.7 %all_to_all.20 = bf16[8,24,768]{2,1,0:T(8,128)(2,1)S(1)} all-to-all(bf16[8,24,768]{2,1,0:T(8,128)(2,1)S(1)} %broadcast_in_dim.6), channel_id=1, replica_groups={{0,64,128,192,256,320,384,448},{1,449,385,321,257,193,129,65},{66,130,1..., dimensions={0} | all-to-all | bytes 589824 | tf_op jit(solution)/shard_map/all_to_all | solution.py:34
  25.4 4.3 %all-to-all-start.1 = ((bf16[4,8,24,768]{3,2,1,0:T(8,128)(2,1)}), bf16[4,8,24,768]{3,2,1,0:T(8,128)(2,1)}, u32[]{:S(2)}, u32[]{:S(2)}) async-start(bf16[4,8,24,768]{3,2,1,0:T(8,128)(2,1)} %broadcast_in_dim.7), calls=%async_computation.1 | async-start | bytes 2359296 | tf_op jit(solution)/shard_map/all_to_all | solution.py:38
  33.7 10.8 %all-to-all-done.1 = bf16[4,8,24,768]{3,2,1,0:T(8,128)(2,1)} async-done(((bf16[4,8,24,768]{3,2,1,0:T(8,128)(2,1)}), bf16[4,8,24,768]{3,2,1,0:T(8,128)(2,1)}, u32[]{:S(2)}, u32[]{:S(2)}) %all-to-all-start.1) | async-done | bytes 1179680 | tf_op jit(solution)/shard_map/all_to_all | solution.py:38
  47.0 1.9 %collective-permute-start.1 = (bf16[4,96,1536]{2,1,0:T(8,128)(2,1)S(1)}, bf16[4,96,1536]{2,1,0:T(8,128)(2,1)S(1)}, u32[]{:S(2)}, u32[]{:S(2)}) collective-permute-start(bf16[4,96,1536]{2,1,0:T(8,128)(2,1)S(1)} %bitcast.43), channel_id=1, source_target_pairs={{0,1},{1,0},{2,3},{3,2},{4,5},{5,4},{6,7},{7,6},{8,9},{9,8},{10,11... | collective-permute-start | bytes 3538952 | tf_op jit(solution)/shard_map/ppermute | solution.py:46
  52.0 4.3 %collective-permute-start.2 = (bf16[192,1536]{1,0:T(8,128)(2,1)S(1)}, bf16[192,1536]{1,0:T(8,128)(2,1)S(1)}, u32[]{:S(2)}, u32[]{:S(2)}) collective-permute-start(bf16[192,1536]{1,0:T(8,128)(2,1)S(1)} %pad_maximum_fusion), channel_id=1, source_target_pairs={{0,2},{1,15},{2,4},{3,1},{4,6},{5,3},{6,8},{7,5},{8,10},{9,7},{10,... | collective-permute-start | bytes 1769480 | tf_op jit(solution)/shard_map/ppermute | solution.py:54
  56.4 4.7 %collective-permute-start.3 = (bf16[96,768]{1,0:T(8,128)(2,1)S(1)}, bf16[96,768]{1,0:T(8,128)(2,1)S(1)}, u32[]{:S(2)}, u32[]{:S(2)}) collective-permute-start(bf16[96,768]{1,0:T(8,128)(2,1)S(1)} %fusion.13), channel_id=1, source_target_pairs={{0,4},{1,13},{2,6},{3,15},{4,8},{5,1},{6,10},{7,3},{8,12},{9,5},{1... | collective-permute-start | bytes 442376 | tf_op jit(solution)/shard_map/ppermute | solution.py:54
  61.1 6.8 %collective-permute-done.3 = bf16[96,768]{1,0:T(8,128)(2,1)S(1)} collective-permute-done((bf16[96,768]{1,0:T(8,128)(2,1)S(1)}, bf16[96,768]{1,0:T(8,128)(2,1)S(1)}, u32[]{:S(2)}, u32[]{:S(2)}) %collective-permute-start.3) | collective-permute-done | bytes 147488 | tf_op jit(solution)/shard_map/ppermute | solution.py:54
  68.1 4.4 %collective-permute-start.4 = (bf16[96,1536]{1,0:T(8,128)(2,1)S(1)}, bf16[96,1536]{1,0:T(8,128)(2,1)S(1)}, u32[]{:S(2)}, u32[]{:S(2)}) collective-permute-start(bf16[96,1536]{1,0:T(8,128)(2,1)S(1)} %fusion.9), channel_id=1, source_target_pairs={{0,4},{1,13},{2,6},{3,15},{4,8},{5,1},{6,10},{7,3},{8,12},{9,5},{1... | collective-permute-start | bytes 884744 | tf_op jit(solution)/shard_map/ppermute | solution.py:54
  72.5 8.4 %collective-permute-done.4 = bf16[96,1536]{1,0:T(8,128)(2,1)S(1)} collective-permute-done((bf16[96,1536]{1,0:T(8,128)(2,1)S(1)}, bf16[96,1536]{1,0:T(8,128)(2,1)S(1)}, u32[]{:S(2)}, u32[]{:S(2)}) %collective-permute-start.4) | collective-permute-done | bytes 294944 | tf_op jit(solution)/shard_map/ppermute | solution.py:54
  81.0 1.9 %collective-permute-start.5 = (bf16[96,1536]{1,0:T(8,128)(2,1)S(1)}, bf16[96,1536]{1,0:T(8,128)(2,1)S(1)}, u32[]{:S(2)}, u32[]{:S(2)}) collective-permute-start(bf16[96,1536]{1,0:T(8,128)(2,1)S(1)} %fusion.14), channel_id=1, source_target_pairs={{0,1},{1,0},{2,3},{3,2},{4,5},{5,4},{6,7},{7,6},{8,9},{9,8},{10,11... | collective-permute-start | bytes 884744 | tf_op jit(solution)/shard_map/ppermute | solution.py:46
  85.1 4.3 %collective-permute-start.7 = (bf16[96,1536]{1,0:T(8,128)(2,1)S(1)}, bf16[96,1536]{1,0:T(8,128)(2,1)S(1)}, u32[]{:S(2)}, u32[]{:S(2)}) collective-permute-start(bf16[96,1536]{1,0:T(8,128)(2,1)S(1)} %get-tuple-element.14), channel_id=1, source_target_pairs={{0,4},{1,13},{2,6},{3,15},{4,8},{5,1},{6,10},{7,3},{8,12},{9,5},{1... | collective-permute-start | bytes 884744 | tf_op jit(solution)/shard_map/ppermute | solution.py:54
  89.4 5.8 %collective-permute-start.6 = (bf16[96,1536]{1,0:T(8,128)(2,1)S(1)}, bf16[96,1536]{1,0:T(8,128)(2,1)S(1)}, u32[]{:S(2)}, u32[]{:S(2)}) collective-permute-start(bf16[96,1536]{1,0:T(8,128)(2,1)S(1)} %get-tuple-element.14), channel_id=1, source_target_pairs={{0,2},{1,15},{2,4},{3,1},{4,6},{5,3},{6,8},{7,5},{8,10},{9,7},{10,... | collective-permute-start | bytes 884744 | tf_op jit(solution)/shard_map/ppermute | solution.py:54
  95.8 3.2 %collective-permute-done.7 = bf16[96,1536]{1,0:T(8,128)(2,1)S(1)} collective-permute-done((bf16[96,1536]{1,0:T(8,128)(2,1)S(1)}, bf16[96,1536]{1,0:T(8,128)(2,1)S(1)}, u32[]{:S(2)}, u32[]{:S(2)}) %collective-permute-start.7) | collective-permute-done | bytes 294944 | tf_op jit(solution)/shard_map/ppermute | solution.py:54
  99.1 2.4 %collective-permute-start.9 = (bf16[96,1536]{1,0:T(8,128)(2,1)S(1)}, bf16[96,1536]{1,0:T(8,128)(2,1)S(1)}, u32[]{:S(2)}, u32[]{:S(2)}) collective-permute-start(bf16[96,1536]{1,0:T(8,128)(2,1)S(1)} %collective-permute-done.7), channel_id=1, source_target_pairs={{0,2},{1,15},{2,4},{3,1},{4,6},{5,3},{6,8},{7,5},{8,10},{9,7},{10,... | collective-permute-start | bytes 884744 | tf_op jit(solution)/shard_map/ppermute | solution.py:54
  101.6 5.9 %collective-permute-start.10 = (bf16[96,768]{1,0:T(8,128)(2,1)S(1)}, bf16[96,768]{1,0:T(8,128)(2,1)S(1)}, u32[]{:S(2)}, u32[]{:S(2)}) collective-permute-start(bf16[96,768]{1,0:T(8,128)(2,1)S(1)} %slice_select_fusion.2), channel_id=1, source_target_pairs={{0,4},{1,13},{2,6},{3,15},{4,8},{5,1},{6,10},{7,3},{8,12},{9,5},{1... | collective-permute-start | bytes 442376 | tf_op jit(solution)/shard_map/ppermute | solution.py:54
  107.5 1.9 %collective-permute-start.8 = (bf16[192,1536]{1,0:T(8,128)(2,1)S(1)}, bf16[192,1536]{1,0:T(8,128)(2,1)S(1)}, u32[]{:S(2)}, u32[]{:S(2)}) collective-permute-start(bf16[192,1536]{1,0:T(8,128)(2,1)S(1)} %pad_maximum_fusion.1), channel_id=1, source_target_pairs={{0,1},{1,0},{2,3},{3,2},{4,5},{5,4},{6,7},{7,6},{8,9},{9,8},{10,11... | collective-permute-start | bytes 1769480 | tf_op jit(solution)/shard_map/ppermute | solution.py:46
  109.4 2.9 %collective-permute-done.10 = bf16[96,768]{1,0:T(8,128)(2,1)S(1)} collective-permute-done((bf16[96,768]{1,0:T(8,128)(2,1)S(1)}, bf16[96,768]{1,0:T(8,128)(2,1)S(1)}, u32[]{:S(2)}, u32[]{:S(2)}) %collective-permute-start.10) | collective-permute-done | bytes 147488 | tf_op jit(solution)/shard_map/ppermute | solution.py:54
  112.4 1.9 %collective-permute-start.11 = (bf16[96,2304]{1,0:T(8,128)(2,1)S(1)}, bf16[96,2304]{1,0:T(8,128)(2,1)S(1)}, u32[]{:S(2)}, u32[]{:S(2)}) collective-permute-start(bf16[96,2304]{1,0:T(8,128)(2,1)S(1)} %pad_maximum_fusion.2), channel_id=1, source_target_pairs={{0,1},{1,0},{2,3},{3,2},{4,5},{5,4},{6,7},{7,6},{8,9},{9,8},{10,11... | collective-permute-start | bytes 1327112 | tf_op jit(solution)/shard_map/ppermute | solution.py:46
  116.2 2.0 %convolution_convert_fusion.2 = bf16[768,768]{1,0:T(8,128)(2,1)S(1)} fusion(bf16[768,1536]{1,0:T(8,128)(2,1)S(1)} %constant_dynamic-update-slice_fusion.y_ref, bf16[768,1536]{1,0:T(8,128)(2,1)S(1)} %copy-done), kind=kOutput, calls=%fused_computation.2 | convolution fusion | flops 1812529152 | bytes 5898240 | tf_op jit(solution)/shard_map/dot_general | solution.py:158
  118.4 20.2 %all_to_all.21 = bf16[4,8,24,768]{3,2,1,0:T(8,128)(2,1)} all-to-all(bf16[4,8,24,768]{3,2,1,0:T(8,128)(2,1)S(1)} %bitcast.39), channel_id=1, replica_groups=mesh['z'=8,'x'=4,'y'=8,'c'=2] {'x'}, dimensions={0} | all-to-all | bytes 2359296 | tf_op jit(solution)/shard_map/all_to_all | solution.py:38
  138.6 2.2 %reduce_sum.24 = bf16[8,24,768]{2,1,0:T(8,128)(2,1)} reduce(bf16[4,8,24,768]{3,2,1,0:T(8,128)(2,1)} %all_to_all.21, bf16[]{:T(256)} %constant.3.clone.1), dimensions={0}, to_apply=%region_0.1 | reduce | flops 442368 | bytes 1474562 | tf_op jit(solution)/shard_map/reduce_sum | solution.py:66
  140.8 7.8 %all-to-all-start.3 = ((bf16[8,24,768]{2,1,0:T(8,128)(2,1)}), bf16[8,24,768]{2,1,0:T(8,128)(2,1)}, u32[]{:S(2)}, u32[]{:S(2)}) async-start(bf16[8,24,768]{2,1,0:T(8,128)(2,1)} %reduce_sum.24), calls=%async_computation.3 | async-start | bytes 589824 | tf_op jit(solution)/shard_map/all_to_all | solution.py:34
  150.3 4.5 %shard_map.58 = bf16[768,1536]{1,0:T(8,128)(2,1)} custom-call(bf16[768,768]{1,0:T(8,128)(2,1)S(1)} %bitcast.38, bf16[768,1536]{1,0:T(8,128)(2,1)S(1)} %copy-done.2), custom_call_target="tpu_custom_call" | custom-call | flops 1811939328 | bytes 5898240 | tf_op jit(solution)/shard_map/pallas_call | solution.py:76
  154.8 4.7 %all-to-all-done.3 = bf16[8,24,768]{2,1,0:T(8,128)(2,1)} async-done(((bf16[8,24,768]{2,1,0:T(8,128)(2,1)}), bf16[8,24,768]{2,1,0:T(8,128)(2,1)}, u32[]{:S(2)}, u32[]{:S(2)}) %all-to-all-start.3) | async-done | bytes 294944 | tf_op jit(solution)/shard_map/all_to_all | solution.py:34
  (48 shorter events, 20.2 us)
Async XLA Ops:
  0.6 45.3 %copy-start = (bf16[768,1536]{1,0:T(8,128)(2,1)S(1)}, bf16[768,1536]{1,0:T(8,128)(2,1)}, u32[]{:S(2)}) copy-start(bf16[768,1536]{1,0:T(8,128)(2,1)} %param.4) | copy-start | bytes 7077892
  0.6 29.0 %copy-start.4 = (bf16[48,1536]{1,0:T(8,128)(2,1)S(1)}, bf16[48,1536]{1,0:T(8,128)(2,1)}, u32[]{:S(2)}) copy-start(bf16[48,1536]{1,0:T(8,128)(2,1)} %param.5) | copy-start | bytes 442372
  25.4 19.1 %all-to-all-start.1 = ((bf16[4,8,24,768]{3,2,1,0:T(8,128)(2,1)}), bf16[4,8,24,768]{3,2,1,0:T(8,128)(2,1)}, u32[]{:S(2)}, u32[]{:S(2)}) async-start(bf16[4,8,24,768]{3,2,1,0:T(8,128)(2,1)} %broadcast_in_dim.7), calls=%async_computation.1 | async-start | bytes 2359296 | tf_op jit(solution)/shard_map/all_to_all | solution.py:38
  29.7 3.3 %collective-permute-start = (bf16[48,1536]{1,0:T(8,128)(2,1)S(1)}, bf16[48,1536]{1,0:T(8,128)(2,1)S(1)}, u32[]{:S(2)}, u32[]{:S(2)}) collective-permute-start(bf16[48,1536]{1,0:T(8,128)(2,1)S(1)} %copy-done.4), channel_id=1, source_target_pairs={{0,1},{1,0},{2,3},{3,2},{4,5},{5,4},{6,7},{7,6},{8,9},{9,8},{10,11... | collective-permute-start | bytes 442376 | tf_op jit(solution)/shard_map/ppermute | solution.py:46
  47.0 4.7 %collective-permute-start.1 = (bf16[4,96,1536]{2,1,0:T(8,128)(2,1)S(1)}, bf16[4,96,1536]{2,1,0:T(8,128)(2,1)S(1)}, u32[]{:S(2)}, u32[]{:S(2)}) collective-permute-start(bf16[4,96,1536]{2,1,0:T(8,128)(2,1)S(1)} %bitcast.43), channel_id=1, source_target_pairs={{0,1},{1,0},{2,3},{3,2},{4,5},{5,4},{6,7},{7,6},{8,9},{9,8},{10,11... | collective-permute-start | bytes 3538952 | tf_op jit(solution)/shard_map/ppermute | solution.py:46
  52.0 32.5 %copy-start.3 = (bf16[96,1536]{1,0:T(8,128)(2,1)S(1)}, bf16[96,1536]{1,0:T(8,128)(2,1)}, u32[]{:S(2)}) copy-start(bf16[96,1536]{1,0:T(8,128)(2,1)} %pad_maximum_fusion.3) | copy-start | bytes 884740
  52.0 15.9 %collective-permute-start.2 = (bf16[192,1536]{1,0:T(8,128)(2,1)S(1)}, bf16[192,1536]{1,0:T(8,128)(2,1)S(1)}, u32[]{:S(2)}, u32[]{:S(2)}) collective-permute-start(bf16[192,1536]{1,0:T(8,128)(2,1)S(1)} %pad_maximum_fusion), channel_id=1, source_target_pairs={{0,2},{1,15},{2,4},{3,1},{4,6},{5,3},{6,8},{7,5},{8,10},{9,7},{10,... | collective-permute-start | bytes 1769480 | tf_op jit(solution)/shard_map/ppermute | solution.py:54
  56.4 11.4 %collective-permute-start.3 = (bf16[96,768]{1,0:T(8,128)(2,1)S(1)}, bf16[96,768]{1,0:T(8,128)(2,1)S(1)}, u32[]{:S(2)}, u32[]{:S(2)}) collective-permute-start(bf16[96,768]{1,0:T(8,128)(2,1)S(1)} %fusion.13), channel_id=1, source_target_pairs={{0,4},{1,13},{2,6},{3,15},{4,8},{5,1},{6,10},{7,3},{8,12},{9,5},{1... | collective-permute-start | bytes 442376 | tf_op jit(solution)/shard_map/ppermute | solution.py:54
  68.1 12.8 %collective-permute-start.4 = (bf16[96,1536]{1,0:T(8,128)(2,1)S(1)}, bf16[96,1536]{1,0:T(8,128)(2,1)S(1)}, u32[]{:S(2)}, u32[]{:S(2)}) collective-permute-start(bf16[96,1536]{1,0:T(8,128)(2,1)S(1)} %fusion.9), channel_id=1, source_target_pairs={{0,4},{1,13},{2,6},{3,15},{4,8},{5,1},{6,10},{7,3},{8,12},{9,5},{1... | collective-permute-start | bytes 884744 | tf_op jit(solution)/shard_map/ppermute | solution.py:54
  81.0 3.5 %collective-permute-start.5 = (bf16[96,1536]{1,0:T(8,128)(2,1)S(1)}, bf16[96,1536]{1,0:T(8,128)(2,1)S(1)}, u32[]{:S(2)}, u32[]{:S(2)}) collective-permute-start(bf16[96,1536]{1,0:T(8,128)(2,1)S(1)} %fusion.14), channel_id=1, source_target_pairs={{0,1},{1,0},{2,3},{3,2},{4,5},{5,4},{6,7},{7,6},{8,9},{9,8},{10,11... | collective-permute-start | bytes 884744 | tf_op jit(solution)/shard_map/ppermute | solution.py:46
  85.1 14.0 %collective-permute-start.7 = (bf16[96,1536]{1,0:T(8,128)(2,1)S(1)}, bf16[96,1536]{1,0:T(8,128)(2,1)S(1)}, u32[]{:S(2)}, u32[]{:S(2)}) collective-permute-start(bf16[96,1536]{1,0:T(8,128)(2,1)S(1)} %get-tuple-element.14), channel_id=1, source_target_pairs={{0,4},{1,13},{2,6},{3,15},{4,8},{5,1},{6,10},{7,3},{8,12},{9,5},{1... | collective-permute-start | bytes 884744 | tf_op jit(solution)/shard_map/ppermute | solution.py:54
  89.4 12.2 %collective-permute-start.6 = (bf16[96,1536]{1,0:T(8,128)(2,1)S(1)}, bf16[96,1536]{1,0:T(8,128)(2,1)S(1)}, u32[]{:S(2)}, u32[]{:S(2)}) collective-permute-start(bf16[96,1536]{1,0:T(8,128)(2,1)S(1)} %get-tuple-element.14), channel_id=1, source_target_pairs={{0,2},{1,15},{2,4},{3,1},{4,6},{5,3},{6,8},{7,5},{8,10},{9,7},{10,... | collective-permute-start | bytes 884744 | tf_op jit(solution)/shard_map/ppermute | solution.py:54
  99.1 13.3 %collective-permute-start.9 = (bf16[96,1536]{1,0:T(8,128)(2,1)S(1)}, bf16[96,1536]{1,0:T(8,128)(2,1)S(1)}, u32[]{:S(2)}, u32[]{:S(2)}) collective-permute-start(bf16[96,1536]{1,0:T(8,128)(2,1)S(1)} %collective-permute-done.7), channel_id=1, source_target_pairs={{0,2},{1,15},{2,4},{3,1},{4,6},{5,3},{6,8},{7,5},{8,10},{9,7},{10,... | collective-permute-start | bytes 884744 | tf_op jit(solution)/shard_map/ppermute | solution.py:54
  101.6 10.7 %collective-permute-start.10 = (bf16[96,768]{1,0:T(8,128)(2,1)S(1)}, bf16[96,768]{1,0:T(8,128)(2,1)S(1)}, u32[]{:S(2)}, u32[]{:S(2)}) collective-permute-start(bf16[96,768]{1,0:T(8,128)(2,1)S(1)} %slice_select_fusion.2), channel_id=1, source_target_pairs={{0,4},{1,13},{2,6},{3,15},{4,8},{5,1},{6,10},{7,3},{8,12},{9,5},{1... | collective-permute-start | bytes 442376 | tf_op jit(solution)/shard_map/ppermute | solution.py:54
  107.5 6.8 %collective-permute-start.8 = (bf16[192,1536]{1,0:T(8,128)(2,1)S(1)}, bf16[192,1536]{1,0:T(8,128)(2,1)S(1)}, u32[]{:S(2)}, u32[]{:S(2)}) collective-permute-start(bf16[192,1536]{1,0:T(8,128)(2,1)S(1)} %pad_maximum_fusion.1), channel_id=1, source_target_pairs={{0,1},{1,0},{2,3},{3,2},{4,5},{5,4},{6,7},{7,6},{8,9},{9,8},{10,11... | collective-permute-start | bytes 1769480 | tf_op jit(solution)/shard_map/ppermute | solution.py:46
  112.4 3.7 %collective-permute-start.11 = (bf16[96,2304]{1,0:T(8,128)(2,1)S(1)}, bf16[96,2304]{1,0:T(8,128)(2,1)S(1)}, u32[]{:S(2)}, u32[]{:S(2)}) collective-permute-start(bf16[96,2304]{1,0:T(8,128)(2,1)S(1)} %pad_maximum_fusion.2), channel_id=1, source_target_pairs={{0,1},{1,0},{2,3},{3,2},{4,5},{5,4},{6,7},{7,6},{8,9},{9,8},{10,11... | collective-permute-start | bytes 1327112 | tf_op jit(solution)/shard_map/ppermute | solution.py:46
  116.2 2.0 %copy-start.1 = (bf16[768,1536]{1,0:T(8,128)(2,1)}, bf16[768,1536]{1,0:T(8,128)(2,1)S(1)}, u32[]{:S(2)}) copy-start(bf16[768,1536]{1,0:T(8,128)(2,1)S(1)} %constant_dynamic-update-slice_fusion.y_ref) | copy-start | bytes 7077892
  140.8 18.6 %all-to-all-start.3 = ((bf16[8,24,768]{2,1,0:T(8,128)(2,1)}), bf16[8,24,768]{2,1,0:T(8,128)(2,1)}, u32[]{:S(2)}, u32[]{:S(2)}) async-start(bf16[8,24,768]{2,1,0:T(8,128)(2,1)} %reduce_sum.24), calls=%async_computation.3 | async-start | bytes 589824 | tf_op jit(solution)/shard_map/all_to_all | solution.py:34
  148.7 1.7 %copy-start.2 = (bf16[768,1536]{1,0:T(8,128)(2,1)S(1)}, bf16[768,1536]{1,0:T(8,128)(2,1)}, u32[]{:S(2)}) copy-start(bf16[768,1536]{1,0:T(8,128)(2,1)} %copy-done.1) | copy-start | bytes 7077892

commit v4 on v3

--- a/solution.py
+++ b/solution.py
@@ -1,8 +1,6 @@
 import jax
 import jax.numpy as jnp
 from jax import lax
-from jax.experimental import pallas as pl
-from jax.experimental.pallas import tpu as pltpu
 from jax.sharding import Mesh
 from jax.sharding import PartitionSpec as P
 
@@ -66,34 +64,9 @@
     return jnp.sum(f32(x), axis=0)
 
 
-def outer(x, y, columns=256):
-    def kernel(x_ref, y_ref, out_ref):
-        out_ref[...] = lax.dot_general(
-            x_ref[...], y_ref[...], (((0,), (0,)), ((), ())), preferred_element_type=jnp.float32
-        ).astype(out_ref.dtype)
-
-    (rows, left), right = x.shape, y.shape[1]
-    return pl.pallas_call(
-        kernel,
-        grid=(right // columns,),
-        in_specs=[
-            pl.BlockSpec((rows, left), lambda i: (0, 0)),
-            pl.BlockSpec((rows, columns), lambda i: (0, i)),
-        ],
-        out_specs=pl.BlockSpec((left, columns), lambda i: (0, i)),
-        out_shape=jax.ShapeDtypeStruct((left, right), x.dtype),
-        compiler_params=pltpu.CompilerParams(vmem_limit_bytes=16 * 2**20),
-        cost_estimate=pl.CostEstimate(
-            flops=2 * rows * left * right,
-            bytes_accessed=2 * (rows * left + rows * right + left * right),
-            transcendentals=0,
-        ),
-    )(x, y)
-
-
 def body(inputs, weight, cotangent):
-    core = lax.axis_index("c")
-    first = core == 0
+    first = lax.axis_index("c") == 0
+    inputs, first = lax.optimization_barrier((inputs, first))
     tokens, width = inputs.shape
     rows, hidden = cotangent.shape
     half = hidden // 2
@@ -108,28 +81,30 @@
     )
 
     by_z = exchange_z(copies(inputs, Z))
-    by_x = exchange_x(copies(by_z, X).reshape(X, Z, tokens, width))
-    by_x, cotangents = lax.optimization_barrier((by_x, cotangents))
-    gathered = by_x.transpose(1, 0, 2, 3).reshape(Z, block, width)
+    by_x = lax.all_gather(by_z[1:].reshape(-1, width), "x", axis=0, tiled=True)
+    by_x = by_x.reshape(X, Z - 1, tokens, width).transpose(1, 0, 2, 3)
+    gathered = by_x.reshape(Z - 1, block, width)
+    own_x = exchange_x(copies(by_z[0], X)).reshape(1, block, width)
 
     def product(x):
         out = jnp.dot(x.reshape(-1, width), weight, preferred_element_type=jnp.float32)
         return bf16(out).reshape(-1, block, hidden)
 
-    lent = product(gathered[4:8])
+    lent = product(gathered[3:7])
     theirs = swap_cores(lent)
-    mine = product(gathered[0:4])
+    mine = product(gathered[0:3])
     four = send(bf16(half_of(f32(lent[0]) + f32(theirs[0]))), 2)
-    ahead = [bf16(f32(mine[3]) + f32(theirs[1])), bf16(f32(mine[1]) + f32(theirs[3]))]
+    ahead = [bf16(f32(mine[2]) + f32(theirs[1])), bf16(f32(mine[0]) + f32(theirs[3]))]
     ahead = send(jnp.concatenate(ahead, axis=0), 1)
     three, one = ahead[:block], ahead[block:]
-    two = f32(mine[2]) + f32(theirs[2]) + f32(three)
+    four, own_x = lax.optimization_barrier((four, own_x))
+    two = f32(mine[1]) + f32(theirs[2]) + f32(three)
     zero = jnp.zeros_like(four)
     four = jnp.concatenate(
         [jnp.where(first, four, zero), jnp.where(first, zero, four)], axis=1
     )
     two = send(bf16(two + f32(four)), 2)
-    partial = f32(mine[0]) + f32(one) + f32(two)
+    partial = f32(product(own_x)[0]) + f32(one) + f32(two)
     preact = partial + f32(swap_cores(bf16(partial)))
 
     gelu_local, slopes = gelu_parts(preact)
@@ -140,8 +115,9 @@
     one = send(own, 1)
     three = send(two, 1)
     four = half_of(two)
-    early, four, activated = lax.optimization_barrier(
-        (jnp.concatenate([one, two], axis=0), four, activated)
+    turned = jnp.concatenate([own_x, gathered], axis=0).reshape(-1, width).T
+    early, four, activated, turned = lax.optimization_barrier(
+        (jnp.concatenate([one, two], axis=0), four, activated, turned)
     )
     four = send(four, 2)
     early = swap_cores(early)
@@ -160,9 +136,9 @@
         )
     )
     partial = partial.reshape(Z, X, tokens, width).transpose(1, 0, 2, 3)
-    grad_weight = outer(gathered.reshape(-1, width), hidden_grad)
     sums = bf16(total(exchange_x(partial)))
     grad_inputs = bf16(total(exchange_z(sums)))
+    grad_weight = bf16(jnp.dot(turned, hidden_grad, preferred_element_type=jnp.float32))
     return (activated, grad_inputs, grad_weight)
 
 

time: 162 us -> 152 us (0.938)
  blocking collectives: 42.9 us -> 68.3 us
  starting transfers between devices: 53.4 us -> 34.8 us
  waiting for transfers between devices: 43.3 us -> 31.7 us
  matrix products: 4.18 us -> 9.94 us
  Pallas kernels: 4.45 us -> 0 us
  local copies, waits for them, and re-layouts: 5.38 us -> 1.42 us
  other arithmetic: 6.56 us -> 4.5 us
    all_gather x0 -> x1, blocking collectives: none -> 15.6 us  [body(): by_x = lax.all_gather(by_z[1:].reshape(-1, width), 'x', axis=0, tiled=True)]
    ppermute x7, starting transfers between devices: 31.7 us -> 20.2 us  [send(): return lax.ppermute(x, ('y', 'c'), pairs)]
    all_to_all x1 -> x0, waiting for transfers between devices: 10.8 us -> none  [exchange_x(): return lax.all_to_all(x, 'x', 0, 0, tiled=True)]
    all_to_all x1 -> x2, blocking collectives: 20.2 us -> 30.1 us  [exchange_x(): return lax.all_to_all(x, 'x', 0, 0, tiled=True)]
    dot_general x0 -> x1, matrix products: none -> 5.46 us  [body(): jnp.dot(turned, hidden_grad, preferred_element_type=jnp.float32)]
    pallas_call x1 -> x0, Pallas kernels: 4.45 us -> none  [outer(): pl.pallas_call(kernel, grid=(right // columns,), in_specs=[pl.BlockSpec((...]
    all_to_all x1 -> x0, starting transfers between devices: 4.29 us -> none  [exchange_x(): return lax.all_to_all(x, 'x', 0, 0, tiled=True)]
    all_to_all x1, starting transfers between devices: 7.81 us -> 4.96 us  [exchange_z(): lax.all_to_all(x, ALL, 0, 0, tiled=True, axis_index_groups=z_groups())]
  transfers between devices with their start and end apart: 14 -> 13, of which waited for: 11 -> 8; matrix products, arithmetic and copies ran while one was open for 2% -> 6% of each run, Pallas kernels for 3% -> 0%
where the time goes in v4:
time: 152 us
  blocking collectives  68.3 us (45%)
  starting transfers between devices  34.8 us (23%)
  waiting for transfers between devices  31.7 us (21%)
  matrix products  9.94 us (7%)
  other arithmetic  4.5 us (3%)
    all_to_all x2, blocking collectives, exchange_x(): return lax.all_to_all(x, 'x', 0, 0, tiled=True)  30.1 us
    ppermute x7, waiting for transfers between devices, send(): return lax.ppermute(x, ('y', 'c'), pairs)  22.7 us
    all_to_all x1, blocking collectives, exchange_z(): lax.all_to_all(x, ALL, 0, 0, tiled=True, axis_index_groups=z_groups())  22.7 us
    ppermute x7, starting transfers between devices, send(): return lax.ppermute(x, ('y', 'c'), pairs)  20.2 us
    all_gather x1, blocking collectives, body(): by_x = lax.all_gather(by_z[1:].reshape(-1, width), 'x', axis=0, tiled=True)  15.6 us
    ppermute x5, starting transfers between devices, swap_cores(): return lax.ppermute(x, 'c', [(0, 1), (1, 0)])  9.6 us
    dot_general x1, matrix products, body(): jnp.dot(turned, hidden_grad, preferred_element_type=jnp.float32)  5.46 us
    all_to_all x1, waiting for transfers between devices, exchange_z(): lax.all_to_all(x, ALL, 0, 0, tiled=True, axis_index_groups=z_groups())  5.15 us
  transfers between devices with their start and end apart: 13, of which 8 were waited for; matrix products, arithmetic and copies ran while one was open for 6% of the time, Pallas kernels for 0%

profile of v4, /device:TPU:8, one launch (start us, length us, event | category | flops | bytes accessed | tf_op | source)
XLA Modules:
  0.0 151.7 jit_solution(5044948492669893669)
XLA Ops:
  1.6 22.7 %all_to_all.20 = bf16[8,24,768]{2,1,0:T(8,128)(2,1)S(1)} all-to-all(bf16[8,24,768]{2,1,0:T(8,128)(2,1)S(1)} %broadcast_in_dim.16), channel_id=1, replica_groups={{0,64,128,192,256,320,384,448},{1,449,385,321,257,193,129,65},{66,130,1..., dimensions={0} | all-to-all | bytes 589824 | tf_op jit(solution)/shard_map/all_to_all | solution.py:32
  24.3 15.6 %all_gather.3 = bf16[672,768]{1,0:T(8,128)(2,1)S(1)} all-gather(bf16[168,768]{1,0:T(8,128)(2,1)S(1)} %bitcast.61), channel_id=1, replica_groups=mesh['z'=8,'x'=4,'y'=8,'c'=2] {'x'}, dimensions={0}, use_global_device_ids=true | all-gather | bytes 1290240 | tf_op jit(solution)/shard_map/all_gather | solution.py:84
  41.1 1.9 %collective-permute-start.1 = (bf16[4,96,1536]{2,1,0:T(8,128)(2,1)S(1)}, bf16[4,96,1536]{2,1,0:T(8,128)(2,1)S(1)}, u32[]{:S(2)}, u32[]{:S(2)}) collective-permute-start(bf16[4,96,1536]{2,1,0:T(8,128)(2,1)S(1)} %bitcast.64), channel_id=1, source_target_pairs={{0,1},{1,0},{2,3},{3,2},{4,5},{5,4},{6,7},{7,6},{8,9},{9,8},{10,11... | collective-permute-start | bytes 3538952 | tf_op jit(solution)/shard_map/ppermute | solution.py:44
  43.9 1.9 %collective-permute-done.1 = bf16[4,96,1536]{2,1,0:T(8,128)(2,1)S(1)} collective-permute-done((bf16[4,96,1536]{2,1,0:T(8,128)(2,1)S(1)}, bf16[4,96,1536]{2,1,0:T(8,128)(2,1)S(1)}, u32[]{:S(2)}, u32[]{:S(2)}) %collective-permute-start.1) | collective-permute-done | bytes 1179680 | tf_op jit(solution)/shard_map/ppermute | solution.py:44
  46.0 3.0 %collective-permute-start.3 = (bf16[192,1536]{1,0:T(8,128)(2,1)S(1)}, bf16[192,1536]{1,0:T(8,128)(2,1)S(1)}, u32[]{:S(2)}, u32[]{:S(2)}) collective-permute-start(bf16[192,1536]{1,0:T(8,128)(2,1)S(1)} %pad_maximum_fusion.1), channel_id=1, source_target_pairs={{0,2},{1,15},{2,4},{3,1},{4,6},{5,3},{6,8},{7,5},{8,10},{9,7},{10,... | collective-permute-start | bytes 1769480 | tf_op jit(solution)/shard_map/ppermute | solution.py:52
  49.1 3.1 %collective-permute-start.2 = (bf16[96,768]{1,0:T(8,128)(2,1)S(1)}, bf16[96,768]{1,0:T(8,128)(2,1)S(1)}, u32[]{:S(2)}, u32[]{:S(2)}) collective-permute-start(bf16[96,768]{1,0:T(8,128)(2,1)S(1)} %fusion.16), channel_id=1, source_target_pairs={{0,4},{1,13},{2,6},{3,15},{4,8},{5,1},{6,10},{7,3},{8,12},{9,5},{1... | collective-permute-start | bytes 442376 | tf_op jit(solution)/shard_map/ppermute | solution.py:52
  52.3 10.6 %all_to_all.21 = bf16[4,24,768]{2,1,0:T(8,128)(2,1)S(1)} all-to-all(bf16[4,24,768]{2,1,0:T(8,128)(2,1)S(1)} %broadcast_in_dim.18), channel_id=1, replica_groups=mesh['z'=8,'x'=4,'y'=8,'c'=2] {'x'}, dimensions={0} | all-to-all | bytes 294912 | tf_op jit(solution)/shard_map/all_to_all | solution.py:36
  63.1 2.1 %collective-permute-start.4 = (bf16[96,1536]{1,0:T(8,128)(2,1)S(1)}, bf16[96,1536]{1,0:T(8,128)(2,1)S(1)}, u32[]{:S(2)}, u32[]{:S(2)}) collective-permute-start(bf16[96,1536]{1,0:T(8,128)(2,1)S(1)} %fusion.12), channel_id=1, source_target_pairs={{0,4},{1,13},{2,6},{3,15},{4,8},{5,1},{6,10},{7,3},{8,12},{9,5},{1... | collective-permute-start | bytes 884744 | tf_op jit(solution)/shard_map/ppermute | solution.py:52
  65.2 1.9 %collective-permute-start = (bf16[48,1536]{1,0:T(8,128)(2,1)S(1)}, bf16[48,1536]{1,0:T(8,128)(2,1)S(1)}, u32[]{:S(2)}, u32[]{:S(2)}) collective-permute-start(bf16[48,1536]{1,0:T(8,128)(2,1)S(1)} %copy-done.1), channel_id=1, source_target_pairs={{0,1},{1,0},{2,3},{3,2},{4,5},{5,4},{6,7},{7,6},{8,9},{9,8},{10,11... | collective-permute-start | bytes 442376 | tf_op jit(solution)/shard_map/ppermute | solution.py:44
  67.1 9.4 %collective-permute-done.4 = bf16[96,1536]{1,0:T(8,128)(2,1)S(1)} collective-permute-done((bf16[96,1536]{1,0:T(8,128)(2,1)S(1)}, bf16[96,1536]{1,0:T(8,128)(2,1)S(1)}, u32[]{:S(2)}, u32[]{:S(2)}) %collective-permute-start.4) | collective-permute-done | bytes 294944 | tf_op jit(solution)/shard_map/ppermute | solution.py:52
  77.0 1.9 %collective-permute-start.5 = (bf16[96,1536]{1,0:T(8,128)(2,1)S(1)}, bf16[96,1536]{1,0:T(8,128)(2,1)S(1)}, u32[]{:S(2)}, u32[]{:S(2)}) collective-permute-start(bf16[96,1536]{1,0:T(8,128)(2,1)S(1)} %get-tuple-element.30), channel_id=1, source_target_pairs={{0,1},{1,0},{2,3},{3,2},{4,5},{5,4},{6,7},{7,6},{8,9},{9,8},{10,11... | collective-permute-start | bytes 884744 | tf_op jit(solution)/shard_map/ppermute | solution.py:44
  81.0 1.9 %collective-permute-start.7 = (bf16[96,1536]{1,0:T(8,128)(2,1)S(1)}, bf16[96,1536]{1,0:T(8,128)(2,1)S(1)}, u32[]{:S(2)}, u32[]{:S(2)}) collective-permute-start(bf16[96,1536]{1,0:T(8,128)(2,1)S(1)} %get-tuple-element.20), channel_id=1, source_target_pairs={{0,4},{1,13},{2,6},{3,15},{4,8},{5,1},{6,10},{7,3},{8,12},{9,5},{1... | collective-permute-start | bytes 884744 | tf_op jit(solution)/shard_map/ppermute | solution.py:52
  82.9 4.0 %collective-permute-start.6 = (bf16[96,1536]{1,0:T(8,128)(2,1)S(1)}, bf16[96,1536]{1,0:T(8,128)(2,1)S(1)}, u32[]{:S(2)}, u32[]{:S(2)}) collective-permute-start(bf16[96,1536]{1,0:T(8,128)(2,1)S(1)} %get-tuple-element.20), channel_id=1, source_target_pairs={{0,2},{1,15},{2,4},{3,1},{4,6},{5,3},{6,8},{7,5},{8,10},{9,7},{10,... | collective-permute-start | bytes 884744 | tf_op jit(solution)/shard_map/ppermute | solution.py:52
  87.6 5.3 %collective-permute-done.7 = bf16[96,1536]{1,0:T(8,128)(2,1)S(1)} collective-permute-done((bf16[96,1536]{1,0:T(8,128)(2,1)S(1)}, bf16[96,1536]{1,0:T(8,128)(2,1)S(1)}, u32[]{:S(2)}, u32[]{:S(2)}) %collective-permute-start.7) | collective-permute-done | bytes 294944 | tf_op jit(solution)/shard_map/ppermute | solution.py:52
  93.0 2.1 %collective-permute-start.9 = (bf16[96,1536]{1,0:T(8,128)(2,1)S(1)}, bf16[96,1536]{1,0:T(8,128)(2,1)S(1)}, u32[]{:S(2)}, u32[]{:S(2)}) collective-permute-start(bf16[96,1536]{1,0:T(8,128)(2,1)S(1)} %collective-permute-done.7), channel_id=1, source_target_pairs={{0,2},{1,15},{2,4},{3,1},{4,6},{5,3},{6,8},{7,5},{8,10},{9,7},{10,... | collective-permute-start | bytes 884744 | tf_op jit(solution)/shard_map/ppermute | solution.py:52
  95.7 4.0 %collective-permute-start.10 = (bf16[96,768]{1,0:T(8,128)(2,1)S(1)}, bf16[96,768]{1,0:T(8,128)(2,1)S(1)}, u32[]{:S(2)}, u32[]{:S(2)}) collective-permute-start(bf16[96,768]{1,0:T(8,128)(2,1)S(1)} %slice_select_fusion.2), channel_id=1, source_target_pairs={{0,4},{1,13},{2,6},{3,15},{4,8},{5,1},{6,10},{7,3},{8,12},{9,5},{1... | collective-permute-start | bytes 442376 | tf_op jit(solution)/shard_map/ppermute | solution.py:52
  99.7 1.9 %collective-permute-start.8 = (bf16[192,1536]{1,0:T(8,128)(2,1)S(1)}, bf16[192,1536]{1,0:T(8,128)(2,1)S(1)}, u32[]{:S(2)}, u32[]{:S(2)}) collective-permute-start(bf16[192,1536]{1,0:T(8,128)(2,1)S(1)} %pad_maximum_fusion.2), channel_id=1, source_target_pairs={{0,1},{1,0},{2,3},{3,2},{4,5},{5,4},{6,7},{7,6},{8,9},{9,8},{10,11... | collective-permute-start | bytes 1769480 | tf_op jit(solution)/shard_map/ppermute | solution.py:44
  101.6 7.3 %collective-permute-done.10 = bf16[96,768]{1,0:T(8,128)(2,1)S(1)} collective-permute-done((bf16[96,768]{1,0:T(8,128)(2,1)S(1)}, bf16[96,768]{1,0:T(8,128)(2,1)S(1)}, u32[]{:S(2)}, u32[]{:S(2)}) %collective-permute-start.10) | collective-permute-done | bytes 147488 | tf_op jit(solution)/shard_map/ppermute | solution.py:52
  109.0 1.9 %collective-permute-start.11 = (bf16[96,2304]{1,0:T(8,128)(2,1)S(1)}, bf16[96,2304]{1,0:T(8,128)(2,1)S(1)}, u32[]{:S(2)}, u32[]{:S(2)}) collective-permute-start(bf16[96,2304]{1,0:T(8,128)(2,1)S(1)} %pad_maximum_fusion.3), channel_id=1, source_target_pairs={{0,1},{1,0},{2,3},{3,2},{4,5},{5,4},{6,7},{7,6},{8,9},{9,8},{10,11... | collective-permute-start | bytes 1327112 | tf_op jit(solution)/shard_map/ppermute | solution.py:44
  112.9 2.0 %convolution_convert_fusion.4 = bf16[768,768]{1,0:T(8,128)(2,1)S(1)} fusion(bf16[768,1536]{1,0:T(8,128)(2,1)S(1)} %constant_dynamic-update-slice_fusion, bf16[768,1536]{1,0:T(8,128)(2,1)S(1)} %copy-done), kind=kOutput, calls=%fused_computation.7 | convolution fusion | flops 1812529152 | bytes 5898240 | tf_op jit(solution)/shard_map/dot_general | solution.py:134
  115.0 19.5 %all_to_all.22 = bf16[4,8,24,768]{3,2,1,0:T(8,128)(2,1)S(1)} all-to-all(bf16[4,8,24,768]{3,2,1,0:T(8,128)(2,1)S(1)} %bitcast.55), channel_id=1, replica_groups=mesh['z'=8,'x'=4,'y'=8,'c'=2] {'x'}, dimensions={0} | all-to-all | bytes 2359296 | tf_op jit(solution)/shard_map/all_to_all | solution.py:36
  135.5 5.0 %all-to-all-start.3 = ((bf16[8,24,768]{2,1,0:T(8,128)(2,1)}), bf16[8,24,768]{2,1,0:T(8,128)(2,1)S(1)}, u32[]{:S(2)}, u32[]{:S(2)}) async-start(bf16[8,24,768]{2,1,0:T(8,128)(2,1)} %reduce_sum.24), calls=%async_computation.3 | async-start | bytes 589824 | tf_op jit(solution)/shard_map/all_to_all | solution.py:32
  140.4 5.5 %convolution_convert_fusion = bf16[768,1536]{1,0:T(8,128)(2,1)} fusion(bf16[768,768]{0,1:T(8,128)(2,1)} %bitcast.59, bf16[768,1536]{1,0:T(8,128)(2,1)} %copy-done.2), kind=kOutput, calls=%fused_computation | convolution fusion | flops 1813118976 | bytes 5898240 | tf_op jit(solution)/shard_map/dot_general | solution.py:141
  145.9 5.1 %all-to-all-done.3 = bf16[8,24,768]{2,1,0:T(8,128)(2,1)S(1)} async-done(((bf16[8,24,768]{2,1,0:T(8,128)(2,1)}), bf16[8,24,768]{2,1,0:T(8,128)(2,1)S(1)}, u32[]{:S(2)}, u32[]{:S(2)}) %all-to-all-start.3) | async-done | bytes 294944 | tf_op jit(solution)/shard_map/all_to_all | solution.py:32
  (49 shorter events, 11.0 us)
Async XLA Ops:
  0.6 39.3 %copy-start = (bf16[768,1536]{1,0:T(8,128)(2,1)S(1)}, bf16[768,1536]{1,0:T(8,128)(2,1)}, u32[]{:S(2)}) copy-start(bf16[768,1536]{1,0:T(8,128)(2,1)} %param.4) | copy-start | bytes 7077892
  41.1 4.7 %collective-permute-start.1 = (bf16[4,96,1536]{2,1,0:T(8,128)(2,1)S(1)}, bf16[4,96,1536]{2,1,0:T(8,128)(2,1)S(1)}, u32[]{:S(2)}, u32[]{:S(2)}) collective-permute-start(bf16[4,96,1536]{2,1,0:T(8,128)(2,1)S(1)} %bitcast.64), channel_id=1, source_target_pairs={{0,1},{1,0},{2,3},{3,2},{4,5},{5,4},{6,7},{7,6},{8,9},{9,8},{10,11... | collective-permute-start | bytes 3538952 | tf_op jit(solution)/shard_map/ppermute | solution.py:44
  45.9 19.2 %copy-start.1 = (bf16[48,1536]{1,0:T(8,128)(2,1)S(1)}, bf16[48,1536]{1,0:T(8,128)(2,1)}, u32[]{:S(2)}) copy-start(bf16[48,1536]{1,0:T(8,128)(2,1)} %param.5) | copy-start | bytes 442372
  46.0 16.9 %collective-permute-start.3 = (bf16[192,1536]{1,0:T(8,128)(2,1)S(1)}, bf16[192,1536]{1,0:T(8,128)(2,1)S(1)}, u32[]{:S(2)}, u32[]{:S(2)}) collective-permute-start(bf16[192,1536]{1,0:T(8,128)(2,1)S(1)} %pad_maximum_fusion.1), channel_id=1, source_target_pairs={{0,2},{1,15},{2,4},{3,1},{4,6},{5,3},{6,8},{7,5},{8,10},{9,7},{10,... | collective-permute-start | bytes 1769480 | tf_op jit(solution)/shard_map/ppermute | solution.py:52
  49.1 13.7 %collective-permute-start.2 = (bf16[96,768]{1,0:T(8,128)(2,1)S(1)}, bf16[96,768]{1,0:T(8,128)(2,1)S(1)}, u32[]{:S(2)}, u32[]{:S(2)}) collective-permute-start(bf16[96,768]{1,0:T(8,128)(2,1)S(1)} %fusion.16), channel_id=1, source_target_pairs={{0,4},{1,13},{2,6},{3,15},{4,8},{5,1},{6,10},{7,3},{8,12},{9,5},{1... | collective-permute-start | bytes 442376 | tf_op jit(solution)/shard_map/ppermute | solution.py:52
  63.1 13.4 %collective-permute-start.4 = (bf16[96,1536]{1,0:T(8,128)(2,1)S(1)}, bf16[96,1536]{1,0:T(8,128)(2,1)S(1)}, u32[]{:S(2)}, u32[]{:S(2)}) collective-permute-start(bf16[96,1536]{1,0:T(8,128)(2,1)S(1)} %fusion.12), channel_id=1, source_target_pairs={{0,4},{1,13},{2,6},{3,15},{4,8},{5,1},{6,10},{7,3},{8,12},{9,5},{1... | collective-permute-start | bytes 884744 | tf_op jit(solution)/shard_map/ppermute | solution.py:52
  65.2 13.8 %collective-permute-start = (bf16[48,1536]{1,0:T(8,128)(2,1)S(1)}, bf16[48,1536]{1,0:T(8,128)(2,1)S(1)}, u32[]{:S(2)}, u32[]{:S(2)}) collective-permute-start(bf16[48,1536]{1,0:T(8,128)(2,1)S(1)} %copy-done.1), channel_id=1, source_target_pairs={{0,1},{1,0},{2,3},{3,2},{4,5},{5,4},{6,7},{7,6},{8,9},{9,8},{10,11... | collective-permute-start | bytes 442376 | tf_op jit(solution)/shard_map/ppermute | solution.py:44
  77.0 3.5 %collective-permute-start.5 = (bf16[96,1536]{1,0:T(8,128)(2,1)S(1)}, bf16[96,1536]{1,0:T(8,128)(2,1)S(1)}, u32[]{:S(2)}, u32[]{:S(2)}) collective-permute-start(bf16[96,1536]{1,0:T(8,128)(2,1)S(1)} %get-tuple-element.30), channel_id=1, source_target_pairs={{0,1},{1,0},{2,3},{3,2},{4,5},{5,4},{6,7},{7,6},{8,9},{9,8},{10,11... | collective-permute-start | bytes 884744 | tf_op jit(solution)/shard_map/ppermute | solution.py:44
  81.0 12.0 %collective-permute-start.7 = (bf16[96,1536]{1,0:T(8,128)(2,1)S(1)}, bf16[96,1536]{1,0:T(8,128)(2,1)S(1)}, u32[]{:S(2)}, u32[]{:S(2)}) collective-permute-start(bf16[96,1536]{1,0:T(8,128)(2,1)S(1)} %get-tuple-element.20), channel_id=1, source_target_pairs={{0,4},{1,13},{2,6},{3,15},{4,8},{5,1},{6,10},{7,3},{8,12},{9,5},{1... | collective-permute-start | bytes 884744 | tf_op jit(solution)/shard_map/ppermute | solution.py:52
  82.9 12.7 %collective-permute-start.6 = (bf16[96,1536]{1,0:T(8,128)(2,1)S(1)}, bf16[96,1536]{1,0:T(8,128)(2,1)S(1)}, u32[]{:S(2)}, u32[]{:S(2)}) collective-permute-start(bf16[96,1536]{1,0:T(8,128)(2,1)S(1)} %get-tuple-element.20), channel_id=1, source_target_pairs={{0,2},{1,15},{2,4},{3,1},{4,6},{5,3},{6,8},{7,5},{8,10},{9,7},{10,... | collective-permute-start | bytes 884744 | tf_op jit(solution)/shard_map/ppermute | solution.py:52
  93.0 16.0 %collective-permute-start.9 = (bf16[96,1536]{1,0:T(8,128)(2,1)S(1)}, bf16[96,1536]{1,0:T(8,128)(2,1)S(1)}, u32[]{:S(2)}, u32[]{:S(2)}) collective-permute-start(bf16[96,1536]{1,0:T(8,128)(2,1)S(1)} %collective-permute-done.7), channel_id=1, source_target_pairs={{0,2},{1,15},{2,4},{3,1},{4,6},{5,3},{6,8},{7,5},{8,10},{9,7},{10,... | collective-permute-start | bytes 884744 | tf_op jit(solution)/shard_map/ppermute | solution.py:52
  95.7 13.3 %collective-permute-start.10 = (bf16[96,768]{1,0:T(8,128)(2,1)S(1)}, bf16[96,768]{1,0:T(8,128)(2,1)S(1)}, u32[]{:S(2)}, u32[]{:S(2)}) collective-permute-start(bf16[96,768]{1,0:T(8,128)(2,1)S(1)} %slice_select_fusion.2), channel_id=1, source_target_pairs={{0,4},{1,13},{2,6},{3,15},{4,8},{5,1},{6,10},{7,3},{8,12},{9,5},{1... | collective-permute-start | bytes 442376 | tf_op jit(solution)/shard_map/ppermute | solution.py:52
  99.7 11.2 %collective-permute-start.8 = (bf16[192,1536]{1,0:T(8,128)(2,1)S(1)}, bf16[192,1536]{1,0:T(8,128)(2,1)S(1)}, u32[]{:S(2)}, u32[]{:S(2)}) collective-permute-start(bf16[192,1536]{1,0:T(8,128)(2,1)S(1)} %pad_maximum_fusion.2), channel_id=1, source_target_pairs={{0,1},{1,0},{2,3},{3,2},{4,5},{5,4},{6,7},{7,6},{8,9},{9,8},{10,11... | collective-permute-start | bytes 1769480 | tf_op jit(solution)/shard_map/ppermute | solution.py:44
  109.0 3.7 %collective-permute-start.11 = (bf16[96,2304]{1,0:T(8,128)(2,1)S(1)}, bf16[96,2304]{1,0:T(8,128)(2,1)S(1)}, u32[]{:S(2)}, u32[]{:S(2)}) collective-permute-start(bf16[96,2304]{1,0:T(8,128)(2,1)S(1)} %pad_maximum_fusion.3), channel_id=1, source_target_pairs={{0,1},{1,0},{2,3},{3,2},{4,5},{5,4},{6,7},{7,6},{8,9},{9,8},{10,11... | collective-permute-start | bytes 1327112 | tf_op jit(solution)/shard_map/ppermute | solution.py:44
  112.9 2.0 %copy-start.2 = (bf16[768,1536]{1,0:T(8,128)(2,1)}, bf16[768,1536]{1,0:T(8,128)(2,1)S(1)}, u32[]{:S(2)}) copy-start(bf16[768,1536]{1,0:T(8,128)(2,1)S(1)} %constant_dynamic-update-slice_fusion) | copy-start | bytes 7077892
  135.5 15.6 %all-to-all-start.3 = ((bf16[8,24,768]{2,1,0:T(8,128)(2,1)}), bf16[8,24,768]{2,1,0:T(8,128)(2,1)S(1)}, u32[]{:S(2)}, u32[]{:S(2)}) async-start(bf16[8,24,768]{2,1,0:T(8,128)(2,1)} %reduce_sum.24), calls=%async_computation.3 | async-start | bytes 589824 | tf_op jit(solution)/shard_map/all_to_all | solution.py:32

commit v5 on v4

--- a/solution.py
+++ b/solution.py
@@ -75,11 +75,6 @@
     def half_of(x):
         return jnp.where(first, x[:, :half], x[:, half:])
 
-    other = swap_cores(cotangent)
-    cotangents = jnp.concatenate(
-        [jnp.where(first, cotangent, other), jnp.where(first, other, cotangent)], axis=0
-    )
-
     by_z = exchange_z(copies(inputs, Z))
     by_x = lax.all_gather(by_z[1:].reshape(-1, width), "x", axis=0, tiled=True)
     by_x = by_x.reshape(X, Z - 1, tokens, width).transpose(1, 0, 2, 3)
@@ -94,10 +89,8 @@
     theirs = swap_cores(lent)
     mine = product(gathered[0:3])
     four = send(bf16(half_of(f32(lent[0]) + f32(theirs[0]))), 2)
-    ahead = [bf16(f32(mine[2]) + f32(theirs[1])), bf16(f32(mine[0]) + f32(theirs[3]))]
-    ahead = send(jnp.concatenate(ahead, axis=0), 1)
-    three, one = ahead[:block], ahead[block:]
-    four, own_x = lax.optimization_barrier((four, own_x))
+    three = send(bf16(f32(mine[2]) + f32(theirs[1])), 1)
+    one = send(bf16(f32(mine[0]) + f32(theirs[3])), 1)
     two = f32(mine[1]) + f32(theirs[2]) + f32(three)
     zero = jnp.zeros_like(four)
     four = jnp.concatenate(
@@ -105,7 +98,12 @@
     )
     two = send(bf16(two + f32(four)), 2)
     partial = f32(product(own_x)[0]) + f32(one) + f32(two)
-    preact = partial + f32(swap_cores(bf16(partial)))
+    other = swap_cores(jnp.concatenate([bf16(partial), cotangent], axis=0))
+    preact = partial + f32(other[:block])
+    other = other[block:]
+    cotangents = jnp.concatenate(
+        [jnp.where(first, cotangent, other), jnp.where(first, other, cotangent)], axis=0
+    )
 
     gelu_local, slopes = gelu_parts(preact)
     activated = bf16(jnp.where(first, gelu_local[:rows], gelu_local[rows:]))

time: 152 us -> 150 us (0.987)
  the two profiles are of different devices: /device:TPU:8 before, /device:TPU:2 now
where the time goes in v5:
time: 150 us; the launch traced here: 149 us
  blocking collectives  65 us (43%)
  starting transfers between devices  39.5 us (26%)
  waiting for transfers between devices  27.4 us (18%)
  matrix products  9.94 us (7%)
  other arithmetic  4.57 us (3%)
    all_to_all x2, blocking collectives, exchange_x(): return lax.all_to_all(x, 'x', 0, 0, tiled=True)  28.2 us
    ppermute x8, starting transfers between devices, send(): return lax.ppermute(x, ('y', 'c'), pairs)  27.5 us
    all_to_all x1, blocking collectives, exchange_z(): lax.all_to_all(x, ALL, 0, 0, tiled=True, axis_index_groups=z_groups())  22.6 us
    ppermute x8, waiting for transfers between devices, send(): return lax.ppermute(x, ('y', 'c'), pairs)  17.2 us
    all_gather x1, blocking collectives, body(): by_x = lax.all_gather(by_z[1:].reshape(-1, width), 'x', axis=0, tiled=True)  14.1 us
    ppermute x4, starting transfers between devices, swap_cores(): return lax.ppermute(x, 'c', [(0, 1), (1, 0)])  7.68 us
    all_to_all x1, waiting for transfers between devices, exchange_z(): lax.all_to_all(x, ALL, 0, 0, tiled=True, axis_index_groups=z_groups())  6.12 us
    dot_general x1, matrix products, body(): jnp.dot(turned, hidden_grad, preferred_element_type=jnp.float32)  5.46 us
  transfers between devices with their start and end apart: 13, of which 8 were waited for; matrix products, arithmetic and copies ran while one was open for 6% of the time, Pallas kernels for 0%

profile of v5, /device:TPU:2, one launch (start us, length us, event | category | flops | bytes accessed | tf_op | source)
XLA Modules:
  0.0 148.9 jit_solution(10769673664327134322)
XLA Ops:
  1.6 22.6 %all_to_all.20 = bf16[8,24,768]{2,1,0:T(8,128)(2,1)S(1)} all-to-all(bf16[8,24,768]{2,1,0:T(8,128)(2,1)S(1)} %broadcast_in_dim.16), channel_id=1, replica_groups={{0,64,128,192,256,320,384,448},{1,449,385,321,257,193,129,65},{66,130,1..., dimensions={0} | all-to-all | bytes 589824 | tf_op jit(solution)/shard_map/all_to_all | solution.py:32
  24.3 14.1 %all_gather.3 = bf16[672,768]{1,0:T(8,128)(2,1)S(1)} all-gather(bf16[168,768]{1,0:T(8,128)(2,1)S(1)} %bitcast.58), channel_id=1, replica_groups=mesh['z'=8,'x'=4,'y'=8,'c'=2] {'x'}, dimensions={0}, use_global_device_ids=true | all-gather | bytes 1290240 | tf_op jit(solution)/shard_map/all_gather | solution.py:79
  39.6 1.9 %collective-permute-start = (bf16[4,96,1536]{2,1,0:T(8,128)(2,1)S(1)}, bf16[4,96,1536]{2,1,0:T(8,128)(2,1)S(1)}, u32[]{:S(2)}, u32[]{:S(2)}) collective-permute-start(bf16[4,96,1536]{2,1,0:T(8,128)(2,1)S(1)} %bitcast.61), channel_id=1, source_target_pairs={{0,1},{1,0},{2,3},{3,2},{4,5},{5,4},{6,7},{7,6},{8,9},{9,8},{10,11... | collective-permute-start | bytes 3538952 | tf_op jit(solution)/shard_map/ppermute | solution.py:44
  42.4 1.9 %collective-permute-done = bf16[4,96,1536]{2,1,0:T(8,128)(2,1)S(1)} collective-permute-done((bf16[4,96,1536]{2,1,0:T(8,128)(2,1)S(1)}, bf16[4,96,1536]{2,1,0:T(8,128)(2,1)S(1)}, u32[]{:S(2)}, u32[]{:S(2)}) %collective-permute-start) | collective-permute-done | bytes 1179680 | tf_op jit(solution)/shard_map/ppermute | solution.py:44
  44.4 5.1 %collective-permute-start.3 = (bf16[96,768]{1,0:T(8,128)(2,1)S(1)}, bf16[96,768]{1,0:T(8,128)(2,1)S(1)}, u32[]{:S(2)}, u32[]{:S(2)}) collective-permute-start(bf16[96,768]{1,0:T(8,128)(2,1)S(1)} %fusion.14), channel_id=1, source_target_pairs={{0,4},{1,13},{2,6},{3,15},{4,8},{5,1},{6,10},{7,3},{8,12},{9,5},{1... | collective-permute-start | bytes 442376 | tf_op jit(solution)/shard_map/ppermute | solution.py:52
  49.6 4.0 %collective-permute-start.2 = (bf16[96,1536]{1,0:T(8,128)(2,1)S(1)}, bf16[96,1536]{1,0:T(8,128)(2,1)S(1)}, u32[]{:S(2)}, u32[]{:S(2)}) collective-permute-start(bf16[96,1536]{1,0:T(8,128)(2,1)S(1)} %get-tuple-element.18), channel_id=1, source_target_pairs={{0,2},{1,15},{2,4},{3,1},{4,6},{5,3},{6,8},{7,5},{8,10},{9,7},{10,... | collective-permute-start | bytes 884744 | tf_op jit(solution)/shard_map/ppermute | solution.py:52
  53.7 2.6 %collective-permute-start.1 = (bf16[96,1536]{1,0:T(8,128)(2,1)S(1)}, bf16[96,1536]{1,0:T(8,128)(2,1)S(1)}, u32[]{:S(2)}, u32[]{:S(2)}) collective-permute-start(bf16[96,1536]{1,0:T(8,128)(2,1)S(1)} %get-tuple-element.17), channel_id=1, source_target_pairs={{0,2},{1,15},{2,4},{3,1},{4,6},{5,3},{6,8},{7,5},{8,10},{9,7},{10,... | collective-permute-start | bytes 884744 | tf_op jit(solution)/shard_map/ppermute | solution.py:52
  56.3 3.1 %collective-permute-done.2 = bf16[96,1536]{1,0:T(8,128)(2,1)S(1)} collective-permute-done((bf16[96,1536]{1,0:T(8,128)(2,1)S(1)}, bf16[96,1536]{1,0:T(8,128)(2,1)S(1)}, u32[]{:S(2)}, u32[]{:S(2)}) %collective-permute-start.2) | collective-permute-done | bytes 294944 | tf_op jit(solution)/shard_map/ppermute | solution.py:52
  59.6 3.1 %collective-permute-start.4 = (bf16[96,1536]{1,0:T(8,128)(2,1)S(1)}, bf16[96,1536]{1,0:T(8,128)(2,1)S(1)}, u32[]{:S(2)}, u32[]{:S(2)}) collective-permute-start(bf16[96,1536]{1,0:T(8,128)(2,1)S(1)} %fusion.11), channel_id=1, source_target_pairs={{0,4},{1,13},{2,6},{3,15},{4,8},{5,1},{6,10},{7,3},{8,12},{9,5},{1... | collective-permute-start | bytes 884744 | tf_op jit(solution)/shard_map/ppermute | solution.py:52
  62.8 8.9 %all_to_all.21 = bf16[4,24,768]{2,1,0:T(8,128)(2,1)S(1)} all-to-all(bf16[4,24,768]{2,1,0:T(8,128)(2,1)S(1)} %broadcast_in_dim.18), channel_id=1, replica_groups=mesh['z'=8,'x'=4,'y'=8,'c'=2] {'x'}, dimensions={0} | all-to-all | bytes 294912 | tf_op jit(solution)/shard_map/all_to_all | solution.py:36
  73.3 1.9 %collective-permute-start.5 = (bf16[144,1536]{1,0:T(8,128)(2,1)S(1)}, bf16[144,1536]{1,0:T(8,128)(2,1)S(1)}, u32[]{:S(2)}, u32[]{:S(2)}) collective-permute-start(bf16[144,1536]{1,0:T(8,128)(2,1)S(1)} %pad_maximum_fusion.2), channel_id=1, source_target_pairs={{0,1},{1,0},{2,3},{3,2},{4,5},{5,4},{6,7},{7,6},{8,9},{9,8},{10,11... | collective-permute-start | bytes 1327112 | tf_op jit(solution)/shard_map/ppermute | solution.py:44
  77.6 3.2 %collective-permute-start.7 = (bf16[96,1536]{1,0:T(8,128)(2,1)S(1)}, bf16[96,1536]{1,0:T(8,128)(2,1)S(1)}, u32[]{:S(2)}, u32[]{:S(2)}) collective-permute-start(bf16[96,1536]{1,0:T(8,128)(2,1)S(1)} %get-tuple-element.16), channel_id=1, source_target_pairs={{0,4},{1,13},{2,6},{3,15},{4,8},{5,1},{6,10},{7,3},{8,12},{9,5},{1... | collective-permute-start | bytes 884744 | tf_op jit(solution)/shard_map/ppermute | solution.py:52
  80.9 2.7 %collective-permute-start.6 = (bf16[96,1536]{1,0:T(8,128)(2,1)S(1)}, bf16[96,1536]{1,0:T(8,128)(2,1)S(1)}, u32[]{:S(2)}, u32[]{:S(2)}) collective-permute-start(bf16[96,1536]{1,0:T(8,128)(2,1)S(1)} %get-tuple-element.16), channel_id=1, source_target_pairs={{0,2},{1,15},{2,4},{3,1},{4,6},{5,3},{6,8},{7,5},{8,10},{9,7},{10,... | collective-permute-start | bytes 884744 | tf_op jit(solution)/shard_map/ppermute | solution.py:52
  84.3 6.2 %collective-permute-done.7 = bf16[96,1536]{1,0:T(8,128)(2,1)S(1)} collective-permute-done((bf16[96,1536]{1,0:T(8,128)(2,1)S(1)}, bf16[96,1536]{1,0:T(8,128)(2,1)S(1)}, u32[]{:S(2)}, u32[]{:S(2)}) %collective-permute-start.7) | collective-permute-done | bytes 294944 | tf_op jit(solution)/shard_map/ppermute | solution.py:52
  90.4 4.8 %collective-permute-start.9 = (bf16[96,1536]{1,0:T(8,128)(2,1)S(1)}, bf16[96,1536]{1,0:T(8,128)(2,1)S(1)}, u32[]{:S(2)}, u32[]{:S(2)}) collective-permute-start(bf16[96,1536]{1,0:T(8,128)(2,1)S(1)} %collective-permute-done.7), channel_id=1, source_target_pairs={{0,2},{1,15},{2,4},{3,1},{4,6},{5,3},{6,8},{7,5},{8,10},{9,7},{10,... | collective-permute-start | bytes 884744 | tf_op jit(solution)/shard_map/ppermute | solution.py:52
  95.4 1.9 %collective-permute-start.10 = (bf16[96,768]{1,0:T(8,128)(2,1)S(1)}, bf16[96,768]{1,0:T(8,128)(2,1)S(1)}, u32[]{:S(2)}, u32[]{:S(2)}) collective-permute-start(bf16[96,768]{1,0:T(8,128)(2,1)S(1)} %slice_select_fusion.2), channel_id=1, source_target_pairs={{0,4},{1,13},{2,6},{3,15},{4,8},{5,1},{6,10},{7,3},{8,12},{9,5},{1... | collective-permute-start | bytes 442376 | tf_op jit(solution)/shard_map/ppermute | solution.py:52
  97.3 1.9 %collective-permute-start.8 = (bf16[192,1536]{1,0:T(8,128)(2,1)S(1)}, bf16[192,1536]{1,0:T(8,128)(2,1)S(1)}, u32[]{:S(2)}, u32[]{:S(2)}) collective-permute-start(bf16[192,1536]{1,0:T(8,128)(2,1)S(1)} %pad_maximum_fusion.1), channel_id=1, source_target_pairs={{0,1},{1,0},{2,3},{3,2},{4,5},{5,4},{6,7},{7,6},{8,9},{9,8},{10,11... | collective-permute-start | bytes 1769480 | tf_op jit(solution)/shard_map/ppermute | solution.py:44
  99.2 6.8 %collective-permute-done.10 = bf16[96,768]{1,0:T(8,128)(2,1)S(1)} collective-permute-done((bf16[96,768]{1,0:T(8,128)(2,1)S(1)}, bf16[96,768]{1,0:T(8,128)(2,1)S(1)}, u32[]{:S(2)}, u32[]{:S(2)}) %collective-permute-start.10) | collective-permute-done | bytes 147488 | tf_op jit(solution)/shard_map/ppermute | solution.py:52
  106.0 1.9 %collective-permute-start.11 = (bf16[96,2304]{1,0:T(8,128)(2,1)S(1)}, bf16[96,2304]{1,0:T(8,128)(2,1)S(1)}, u32[]{:S(2)}, u32[]{:S(2)}) collective-permute-start(bf16[96,2304]{1,0:T(8,128)(2,1)S(1)} %pad_maximum_fusion.3), channel_id=1, source_target_pairs={{0,1},{1,0},{2,3},{3,2},{4,5},{5,4},{6,7},{7,6},{8,9},{9,8},{10,11... | collective-permute-start | bytes 1327112 | tf_op jit(solution)/shard_map/ppermute | solution.py:44
  109.9 2.0 %convolution_convert_fusion.4 = bf16[768,768]{1,0:T(8,128)(2,1)S(1)} fusion(bf16[768,1536]{1,0:T(8,128)(2,1)S(1)} %constant_dynamic-update-slice_fusion, bf16[768,1536]{1,0:T(8,128)(2,1)S(1)} %copy-done), kind=kOutput, calls=%fused_computation.5 | convolution fusion | flops 1812529152 | bytes 5898240 | tf_op jit(solution)/shard_map/dot_general | solution.py:132
  112.0 19.3 %all_to_all.22 = bf16[4,8,24,768]{3,2,1,0:T(8,128)(2,1)S(1)} all-to-all(bf16[4,8,24,768]{3,2,1,0:T(8,128)(2,1)S(1)} %bitcast.52), channel_id=1, replica_groups=mesh['z'=8,'x'=4,'y'=8,'c'=2] {'x'}, dimensions={0} | all-to-all | bytes 2359296 | tf_op jit(solution)/shard_map/all_to_all | solution.py:36
  132.3 4.3 %all-to-all-start.3 = ((bf16[8,24,768]{2,1,0:T(8,128)(2,1)}), bf16[8,24,768]{2,1,0:T(8,128)(2,1)S(1)}, u32[]{:S(2)}, u32[]{:S(2)}) async-start(bf16[8,24,768]{2,1,0:T(8,128)(2,1)} %reduce_sum.24), calls=%async_computation.3 | async-start | bytes 589824 | tf_op jit(solution)/shard_map/all_to_all | solution.py:32
  136.7 5.5 %convolution_convert_fusion = bf16[768,1536]{1,0:T(8,128)(2,1)} fusion(bf16[768,768]{0,1:T(8,128)(2,1)} %bitcast.56, bf16[768,1536]{1,0:T(8,128)(2,1)} %copy-done.2), kind=kOutput, calls=%fused_computation | convolution fusion | flops 1813118976 | bytes 5898240 | tf_op jit(solution)/shard_map/dot_general | solution.py:139
  142.1 6.1 %all-to-all-done.3 = bf16[8,24,768]{2,1,0:T(8,128)(2,1)S(1)} async-done(((bf16[8,24,768]{2,1,0:T(8,128)(2,1)}), bf16[8,24,768]{2,1,0:T(8,128)(2,1)S(1)}, u32[]{:S(2)}, u32[]{:S(2)}) %all-to-all-start.3) | async-done | bytes 294944 | tf_op jit(solution)/shard_map/all_to_all | solution.py:32
  (49 shorter events, 11.8 us)
Async XLA Ops:
  0.6 37.9 %copy-start = (bf16[768,1536]{1,0:T(8,128)(2,1)S(1)}, bf16[768,1536]{1,0:T(8,128)(2,1)}, u32[]{:S(2)}) copy-start(bf16[768,1536]{1,0:T(8,128)(2,1)} %param.4) | copy-start | bytes 7077892
  39.6 4.7 %collective-permute-start = (bf16[4,96,1536]{2,1,0:T(8,128)(2,1)S(1)}, bf16[4,96,1536]{2,1,0:T(8,128)(2,1)S(1)}, u32[]{:S(2)}, u32[]{:S(2)}) collective-permute-start(bf16[4,96,1536]{2,1,0:T(8,128)(2,1)S(1)} %bitcast.61), channel_id=1, source_target_pairs={{0,1},{1,0},{2,3},{3,2},{4,5},{5,4},{6,7},{7,6},{8,9},{9,8},{10,11... | collective-permute-start | bytes 3538952 | tf_op jit(solution)/shard_map/ppermute | solution.py:44
  44.4 11.9 %collective-permute-start.3 = (bf16[96,768]{1,0:T(8,128)(2,1)S(1)}, bf16[96,768]{1,0:T(8,128)(2,1)S(1)}, u32[]{:S(2)}, u32[]{:S(2)}) collective-permute-start(bf16[96,768]{1,0:T(8,128)(2,1)S(1)} %fusion.14), channel_id=1, source_target_pairs={{0,4},{1,13},{2,6},{3,15},{4,8},{5,1},{6,10},{7,3},{8,12},{9,5},{1... | collective-permute-start | bytes 442376 | tf_op jit(solution)/shard_map/ppermute | solution.py:52
  49.6 9.8 %collective-permute-start.2 = (bf16[96,1536]{1,0:T(8,128)(2,1)S(1)}, bf16[96,1536]{1,0:T(8,128)(2,1)S(1)}, u32[]{:S(2)}, u32[]{:S(2)}) collective-permute-start(bf16[96,1536]{1,0:T(8,128)(2,1)S(1)} %get-tuple-element.18), channel_id=1, source_target_pairs={{0,2},{1,15},{2,4},{3,1},{4,6},{5,3},{6,8},{7,5},{8,10},{9,7},{10,... | collective-permute-start | bytes 884744 | tf_op jit(solution)/shard_map/ppermute | solution.py:52
  53.7 18.0 %collective-permute-start.1 = (bf16[96,1536]{1,0:T(8,128)(2,1)S(1)}, bf16[96,1536]{1,0:T(8,128)(2,1)S(1)}, u32[]{:S(2)}, u32[]{:S(2)}) collective-permute-start(bf16[96,1536]{1,0:T(8,128)(2,1)S(1)} %get-tuple-element.17), channel_id=1, source_target_pairs={{0,2},{1,15},{2,4},{3,1},{4,6},{5,3},{6,8},{7,5},{8,10},{9,7},{10,... | collective-permute-start | bytes 884744 | tf_op jit(solution)/shard_map/ppermute | solution.py:52
  59.6 13.7 %copy-start.1 = (bf16[48,1536]{1,0:T(8,128)(2,1)S(1)}, bf16[48,1536]{1,0:T(8,128)(2,1)}, u32[]{:S(2)}) copy-start(bf16[48,1536]{1,0:T(8,128)(2,1)} %param.5) | copy-start | bytes 442372
  59.6 13.1 %collective-permute-start.4 = (bf16[96,1536]{1,0:T(8,128)(2,1)S(1)}, bf16[96,1536]{1,0:T(8,128)(2,1)S(1)}, u32[]{:S(2)}, u32[]{:S(2)}) collective-permute-start(bf16[96,1536]{1,0:T(8,128)(2,1)S(1)} %fusion.11), channel_id=1, source_target_pairs={{0,4},{1,13},{2,6},{3,15},{4,8},{5,1},{6,10},{7,3},{8,12},{9,5},{1... | collective-permute-start | bytes 884744 | tf_op jit(solution)/shard_map/ppermute | solution.py:52
  73.3 3.7 %collective-permute-start.5 = (bf16[144,1536]{1,0:T(8,128)(2,1)S(1)}, bf16[144,1536]{1,0:T(8,128)(2,1)S(1)}, u32[]{:S(2)}, u32[]{:S(2)}) collective-permute-start(bf16[144,1536]{1,0:T(8,128)(2,1)S(1)} %pad_maximum_fusion.2), channel_id=1, source_target_pairs={{0,1},{1,0},{2,3},{3,2},{4,5},{5,4},{6,7},{7,6},{8,9},{9,8},{10,11... | collective-permute-start | bytes 1327112 | tf_op jit(solution)/shard_map/ppermute | solution.py:44
  77.6 12.8 %collective-permute-start.7 = (bf16[96,1536]{1,0:T(8,128)(2,1)S(1)}, bf16[96,1536]{1,0:T(8,128)(2,1)S(1)}, u32[]{:S(2)}, u32[]{:S(2)}) collective-permute-start(bf16[96,1536]{1,0:T(8,128)(2,1)S(1)} %get-tuple-element.16), channel_id=1, source_target_pairs={{0,4},{1,13},{2,6},{3,15},{4,8},{5,1},{6,10},{7,3},{8,12},{9,5},{1... | collective-permute-start | bytes 884744 | tf_op jit(solution)/shard_map/ppermute | solution.py:52
  80.9 14.4 %collective-permute-start.6 = (bf16[96,1536]{1,0:T(8,128)(2,1)S(1)}, bf16[96,1536]{1,0:T(8,128)(2,1)S(1)}, u32[]{:S(2)}, u32[]{:S(2)}) collective-permute-start(bf16[96,1536]{1,0:T(8,128)(2,1)S(1)} %get-tuple-element.16), channel_id=1, source_target_pairs={{0,2},{1,15},{2,4},{3,1},{4,6},{5,3},{6,8},{7,5},{8,10},{9,7},{10,... | collective-permute-start | bytes 884744 | tf_op jit(solution)/shard_map/ppermute | solution.py:52
  90.4 15.6 %collective-permute-start.9 = (bf16[96,1536]{1,0:T(8,128)(2,1)S(1)}, bf16[96,1536]{1,0:T(8,128)(2,1)S(1)}, u32[]{:S(2)}, u32[]{:S(2)}) collective-permute-start(bf16[96,1536]{1,0:T(8,128)(2,1)S(1)} %collective-permute-done.7), channel_id=1, source_target_pairs={{0,2},{1,15},{2,4},{3,1},{4,6},{5,3},{6,8},{7,5},{8,10},{9,7},{10,... | collective-permute-start | bytes 884744 | tf_op jit(solution)/shard_map/ppermute | solution.py:52
  95.4 10.6 %collective-permute-start.10 = (bf16[96,768]{1,0:T(8,128)(2,1)S(1)}, bf16[96,768]{1,0:T(8,128)(2,1)S(1)}, u32[]{:S(2)}, u32[]{:S(2)}) collective-permute-start(bf16[96,768]{1,0:T(8,128)(2,1)S(1)} %slice_select_fusion.2), channel_id=1, source_target_pairs={{0,4},{1,13},{2,6},{3,15},{4,8},{5,1},{6,10},{7,3},{8,12},{9,5},{1... | collective-permute-start | bytes 442376 | tf_op jit(solution)/shard_map/ppermute | solution.py:52
  97.3 10.7 %collective-permute-start.8 = (bf16[192,1536]{1,0:T(8,128)(2,1)S(1)}, bf16[192,1536]{1,0:T(8,128)(2,1)S(1)}, u32[]{:S(2)}, u32[]{:S(2)}) collective-permute-start(bf16[192,1536]{1,0:T(8,128)(2,1)S(1)} %pad_maximum_fusion.1), channel_id=1, source_target_pairs={{0,1},{1,0},{2,3},{3,2},{4,5},{5,4},{6,7},{7,6},{8,9},{9,8},{10,11... | collective-permute-start | bytes 1769480 | tf_op jit(solution)/shard_map/ppermute | solution.py:44
  106.0 3.7 %collective-permute-start.11 = (bf16[96,2304]{1,0:T(8,128)(2,1)S(1)}, bf16[96,2304]{1,0:T(8,128)(2,1)S(1)}, u32[]{:S(2)}, u32[]{:S(2)}) collective-permute-start(bf16[96,2304]{1,0:T(8,128)(2,1)S(1)} %pad_maximum_fusion.3), channel_id=1, source_target_pairs={{0,1},{1,0},{2,3},{3,2},{4,5},{5,4},{6,7},{7,6},{8,9},{9,8},{10,11... | collective-permute-start | bytes 1327112 | tf_op jit(solution)/shard_map/ppermute | solution.py:44
  109.9 2.0 %copy-start.2 = (bf16[768,1536]{1,0:T(8,128)(2,1)}, bf16[768,1536]{1,0:T(8,128)(2,1)S(1)}, u32[]{:S(2)}) copy-start(bf16[768,1536]{1,0:T(8,128)(2,1)S(1)} %constant_dynamic-update-slice_fusion) | copy-start | bytes 7077892
  132.3 15.9 %all-to-all-start.3 = ((bf16[8,24,768]{2,1,0:T(8,128)(2,1)}), bf16[8,24,768]{2,1,0:T(8,128)(2,1)S(1)}, u32[]{:S(2)}, u32[]{:S(2)}) async-start(bf16[8,24,768]{2,1,0:T(8,128)(2,1)} %reduce_sum.24), calls=%async_computation.3 | async-start | bytes 589824 | tf_op jit(solution)/shard_map/all_to_all | solution.py:32

commit v6 on v5

--- a/solution.py
+++ b/solution.py
@@ -100,7 +100,7 @@
     partial = f32(product(own_x)[0]) + f32(one) + f32(two)
     other = swap_cores(jnp.concatenate([bf16(partial), cotangent], axis=0))
     preact = partial + f32(other[:block])
-    other = other[block:]
+    other, gathered = lax.optimization_barrier((other[block:], gathered))
     cotangents = jnp.concatenate(
         [jnp.where(first, cotangent, other), jnp.where(first, other, cotangent)], axis=0
     )

time: 150 us -> 150 us (level)
  no operation moved by 1% of the time
where the time goes in v6:
time: 150 us; the launch traced here: 149 us
  blocking collectives  65 us (43%)
  starting transfers between devices  39.5 us (26%)
  waiting for transfers between devices  27.4 us (18%)
  matrix products  9.93 us (7%)
  other arithmetic  4.57 us (3%)
    all_to_all x2, blocking collectives, exchange_x(): return lax.all_to_all(x, 'x', 0, 0, tiled=True)  28.2 us
    ppermute x8, starting transfers between devices, send(): return lax.ppermute(x, ('y', 'c'), pairs)  27.5 us
    all_to_all x1, blocking collectives, exchange_z(): lax.all_to_all(x, ALL, 0, 0, tiled=True, axis_index_groups=z_groups())  22.6 us
    ppermute x8, waiting for transfers between devices, send(): return lax.ppermute(x, ('y', 'c'), pairs)  16 us
    all_gather x1, blocking collectives, body(): by_x = lax.all_gather(by_z[1:].reshape(-1, width), 'x', axis=0, tiled=True)  14.1 us
    ppermute x4, starting transfers between devices, swap_cores(): return lax.ppermute(x, 'c', [(0, 1), (1, 0)])  7.68 us
    all_to_all x1, waiting for transfers between devices, exchange_z(): lax.all_to_all(x, ALL, 0, 0, tiled=True, axis_index_groups=z_groups())  6.13 us
    dot_general x1, matrix products, body(): jnp.dot(turned, hidden_grad, preferred_element_type=jnp.float32)  5.46 us
  transfers between devices with their start and end apart: 13, of which 8 were waited for; matrix products, arithmetic and copies ran while one was open for 6% of the time, Pallas kernels for 0%

profile of v6, /device:TPU:2, one launch (start us, length us, event | category | flops | bytes accessed | tf_op | source)
XLA Modules:
  0.0 148.9 jit_solution(13296566001813063692)
XLA Ops:
  1.6 22.6 %all_to_all.20 = bf16[8,24,768]{2,1,0:T(8,128)(2,1)S(1)} all-to-all(bf16[8,24,768]{2,1,0:T(8,128)(2,1)S(1)} %broadcast_in_dim.16), channel_id=1, replica_groups={{0,64,128,192,256,320,384,448},{1,449,385,321,257,193,129,65},{66,130,1..., dimensions={0} | all-to-all | bytes 589824 | tf_op jit(solution)/shard_map/all_to_all | solution.py:32
  24.3 14.1 %all_gather.3 = bf16[672,768]{1,0:T(8,128)(2,1)S(1)} all-gather(bf16[168,768]{1,0:T(8,128)(2,1)S(1)} %bitcast.58), channel_id=1, replica_groups=mesh['z'=8,'x'=4,'y'=8,'c'=2] {'x'}, dimensions={0}, use_global_device_ids=true | all-gather | bytes 1290240 | tf_op jit(solution)/shard_map/all_gather | solution.py:79
  39.6 1.9 %collective-permute-start = (bf16[4,96,1536]{2,1,0:T(8,128)(2,1)S(1)}, bf16[4,96,1536]{2,1,0:T(8,128)(2,1)S(1)}, u32[]{:S(2)}, u32[]{:S(2)}) collective-permute-start(bf16[4,96,1536]{2,1,0:T(8,128)(2,1)S(1)} %bitcast.61), channel_id=1, source_target_pairs={{0,1},{1,0},{2,3},{3,2},{4,5},{5,4},{6,7},{7,6},{8,9},{9,8},{10,11... | collective-permute-start | bytes 3538952 | tf_op jit(solution)/shard_map/ppermute | solution.py:44
  42.4 1.9 %collective-permute-done = bf16[4,96,1536]{2,1,0:T(8,128)(2,1)S(1)} collective-permute-done((bf16[4,96,1536]{2,1,0:T(8,128)(2,1)S(1)}, bf16[4,96,1536]{2,1,0:T(8,128)(2,1)S(1)}, u32[]{:S(2)}, u32[]{:S(2)}) %collective-permute-start) | collective-permute-done | bytes 1179680 | tf_op jit(solution)/shard_map/ppermute | solution.py:44
  44.4 5.1 %collective-permute-start.3 = (bf16[96,768]{1,0:T(8,128)(2,1)S(1)}, bf16[96,768]{1,0:T(8,128)(2,1)S(1)}, u32[]{:S(2)}, u32[]{:S(2)}) collective-permute-start(bf16[96,768]{1,0:T(8,128)(2,1)S(1)} %fusion.14), channel_id=1, source_target_pairs={{0,4},{1,13},{2,6},{3,15},{4,8},{5,1},{6,10},{7,3},{8,12},{9,5},{1... | collective-permute-start | bytes 442376 | tf_op jit(solution)/shard_map/ppermute | solution.py:52
  49.6 4.0 %collective-permute-start.2 = (bf16[96,1536]{1,0:T(8,128)(2,1)S(1)}, bf16[96,1536]{1,0:T(8,128)(2,1)S(1)}, u32[]{:S(2)}, u32[]{:S(2)}) collective-permute-start(bf16[96,1536]{1,0:T(8,128)(2,1)S(1)} %get-tuple-element.22), channel_id=1, source_target_pairs={{0,2},{1,15},{2,4},{3,1},{4,6},{5,3},{6,8},{7,5},{8,10},{9,7},{10,... | collective-permute-start | bytes 884744 | tf_op jit(solution)/shard_map/ppermute | solution.py:52
  53.7 2.6 %collective-permute-start.1 = (bf16[96,1536]{1,0:T(8,128)(2,1)S(1)}, bf16[96,1536]{1,0:T(8,128)(2,1)S(1)}, u32[]{:S(2)}, u32[]{:S(2)}) collective-permute-start(bf16[96,1536]{1,0:T(8,128)(2,1)S(1)} %get-tuple-element.21), channel_id=1, source_target_pairs={{0,2},{1,15},{2,4},{3,1},{4,6},{5,3},{6,8},{7,5},{8,10},{9,7},{10,... | collective-permute-start | bytes 884744 | tf_op jit(solution)/shard_map/ppermute | solution.py:52
  56.3 3.1 %collective-permute-done.2 = bf16[96,1536]{1,0:T(8,128)(2,1)S(1)} collective-permute-done((bf16[96,1536]{1,0:T(8,128)(2,1)S(1)}, bf16[96,1536]{1,0:T(8,128)(2,1)S(1)}, u32[]{:S(2)}, u32[]{:S(2)}) %collective-permute-start.2) | collective-permute-done | bytes 294944 | tf_op jit(solution)/shard_map/ppermute | solution.py:52
  59.6 3.1 %collective-permute-start.4 = (bf16[96,1536]{1,0:T(8,128)(2,1)S(1)}, bf16[96,1536]{1,0:T(8,128)(2,1)S(1)}, u32[]{:S(2)}, u32[]{:S(2)}) collective-permute-start(bf16[96,1536]{1,0:T(8,128)(2,1)S(1)} %fusion.11), channel_id=1, source_target_pairs={{0,4},{1,13},{2,6},{3,15},{4,8},{5,1},{6,10},{7,3},{8,12},{9,5},{1... | collective-permute-start | bytes 884744 | tf_op jit(solution)/shard_map/ppermute | solution.py:52
  62.8 8.9 %all_to_all.21 = bf16[4,24,768]{2,1,0:T(8,128)(2,1)S(1)} all-to-all(bf16[4,24,768]{2,1,0:T(8,128)(2,1)S(1)} %broadcast_in_dim.18), channel_id=1, replica_groups=mesh['z'=8,'x'=4,'y'=8,'c'=2] {'x'}, dimensions={0} | all-to-all | bytes 294912 | tf_op jit(solution)/shard_map/all_to_all | solution.py:36
  73.3 1.9 %collective-permute-start.5 = (bf16[144,1536]{1,0:T(8,128)(2,1)S(1)}, bf16[144,1536]{1,0:T(8,128)(2,1)S(1)}, u32[]{:S(2)}, u32[]{:S(2)}) collective-permute-start(bf16[144,1536]{1,0:T(8,128)(2,1)S(1)} %pad_maximum_fusion.2), channel_id=1, source_target_pairs={{0,1},{1,0},{2,3},{3,2},{4,5},{5,4},{6,7},{7,6},{8,9},{9,8},{10,11... | collective-permute-start | bytes 1327112 | tf_op jit(solution)/shard_map/ppermute | solution.py:44
  77.6 3.2 %collective-permute-start.7 = (bf16[96,1536]{1,0:T(8,128)(2,1)S(1)}, bf16[96,1536]{1,0:T(8,128)(2,1)S(1)}, u32[]{:S(2)}, u32[]{:S(2)}) collective-permute-start(bf16[96,1536]{1,0:T(8,128)(2,1)S(1)} %get-tuple-element.20), channel_id=1, source_target_pairs={{0,4},{1,13},{2,6},{3,15},{4,8},{5,1},{6,10},{7,3},{8,12},{9,5},{1... | collective-permute-start | bytes 884744 | tf_op jit(solution)/shard_map/ppermute | solution.py:52
  80.9 2.7 %collective-permute-start.6 = (bf16[96,1536]{1,0:T(8,128)(2,1)S(1)}, bf16[96,1536]{1,0:T(8,128)(2,1)S(1)}, u32[]{:S(2)}, u32[]{:S(2)}) collective-permute-start(bf16[96,1536]{1,0:T(8,128)(2,1)S(1)} %get-tuple-element.20), channel_id=1, source_target_pairs={{0,2},{1,15},{2,4},{3,1},{4,6},{5,3},{6,8},{7,5},{8,10},{9,7},{10,... | collective-permute-start | bytes 884744 | tf_op jit(solution)/shard_map/ppermute | solution.py:52
  85.4 5.0 %collective-permute-done.7 = bf16[96,1536]{1,0:T(8,128)(2,1)S(1)} collective-permute-done((bf16[96,1536]{1,0:T(8,128)(2,1)S(1)}, bf16[96,1536]{1,0:T(8,128)(2,1)S(1)}, u32[]{:S(2)}, u32[]{:S(2)}) %collective-permute-start.7) | collective-permute-done | bytes 294944 | tf_op jit(solution)/shard_map/ppermute | solution.py:52
  90.5 4.8 %collective-permute-start.9 = (bf16[96,1536]{1,0:T(8,128)(2,1)S(1)}, bf16[96,1536]{1,0:T(8,128)(2,1)S(1)}, u32[]{:S(2)}, u32[]{:S(2)}) collective-permute-start(bf16[96,1536]{1,0:T(8,128)(2,1)S(1)} %collective-permute-done.7), channel_id=1, source_target_pairs={{0,2},{1,15},{2,4},{3,1},{4,6},{5,3},{6,8},{7,5},{8,10},{9,7},{10,... | collective-permute-start | bytes 884744 | tf_op jit(solution)/shard_map/ppermute | solution.py:52
  95.4 1.9 %collective-permute-start.10 = (bf16[96,768]{1,0:T(8,128)(2,1)S(1)}, bf16[96,768]{1,0:T(8,128)(2,1)S(1)}, u32[]{:S(2)}, u32[]{:S(2)}) collective-permute-start(bf16[96,768]{1,0:T(8,128)(2,1)S(1)} %slice_select_fusion.2), channel_id=1, source_target_pairs={{0,4},{1,13},{2,6},{3,15},{4,8},{5,1},{6,10},{7,3},{8,12},{9,5},{1... | collective-permute-start | bytes 442376 | tf_op jit(solution)/shard_map/ppermute | solution.py:52
  97.3 1.9 %collective-permute-start.8 = (bf16[192,1536]{1,0:T(8,128)(2,1)S(1)}, bf16[192,1536]{1,0:T(8,128)(2,1)S(1)}, u32[]{:S(2)}, u32[]{:S(2)}) collective-permute-start(bf16[192,1536]{1,0:T(8,128)(2,1)S(1)} %pad_maximum_fusion.1), channel_id=1, source_target_pairs={{0,1},{1,0},{2,3},{3,2},{4,5},{5,4},{6,7},{7,6},{8,9},{9,8},{10,11... | collective-permute-start | bytes 1769480 | tf_op jit(solution)/shard_map/ppermute | solution.py:44
  99.2 6.8 %collective-permute-done.10 = bf16[96,768]{1,0:T(8,128)(2,1)S(1)} collective-permute-done((bf16[96,768]{1,0:T(8,128)(2,1)S(1)}, bf16[96,768]{1,0:T(8,128)(2,1)S(1)}, u32[]{:S(2)}, u32[]{:S(2)}) %collective-permute-start.10) | collective-permute-done | bytes 147488 | tf_op jit(solution)/shard_map/ppermute | solution.py:52
  106.0 1.9 %collective-permute-start.11 = (bf16[96,2304]{1,0:T(8,128)(2,1)S(1)}, bf16[96,2304]{1,0:T(8,128)(2,1)S(1)}, u32[]{:S(2)}, u32[]{:S(2)}) collective-permute-start(bf16[96,2304]{1,0:T(8,128)(2,1)S(1)} %pad_maximum_fusion.3), channel_id=1, source_target_pairs={{0,1},{1,0},{2,3},{3,2},{4,5},{5,4},{6,7},{7,6},{8,9},{9,8},{10,11... | collective-permute-start | bytes 1327112 | tf_op jit(solution)/shard_map/ppermute | solution.py:44
  109.9 2.0 %convolution_convert_fusion.4 = bf16[768,768]{1,0:T(8,128)(2,1)S(1)} fusion(bf16[768,1536]{1,0:T(8,128)(2,1)S(1)} %constant_dynamic-update-slice_fusion, bf16[768,1536]{1,0:T(8,128)(2,1)S(1)} %copy-done), kind=kOutput, calls=%fused_computation.5 | convolution fusion | flops 1812529152 | bytes 5898240 | tf_op jit(solution)/shard_map/dot_general | solution.py:132
  112.0 19.3 %all_to_all.22 = bf16[4,8,24,768]{3,2,1,0:T(8,128)(2,1)S(1)} all-to-all(bf16[4,8,24,768]{3,2,1,0:T(8,128)(2,1)S(1)} %bitcast.52), channel_id=1, replica_groups=mesh['z'=8,'x'=4,'y'=8,'c'=2] {'x'}, dimensions={0} | all-to-all | bytes 2359296 | tf_op jit(solution)/shard_map/all_to_all | solution.py:36
  132.3 4.3 %all-to-all-start.3 = ((bf16[8,24,768]{2,1,0:T(8,128)(2,1)}), bf16[8,24,768]{2,1,0:T(8,128)(2,1)S(1)}, u32[]{:S(2)}, u32[]{:S(2)}) async-start(bf16[8,24,768]{2,1,0:T(8,128)(2,1)} %reduce_sum.24), calls=%async_computation.3 | async-start | bytes 589824 | tf_op jit(solution)/shard_map/all_to_all | solution.py:32
  136.7 5.5 %convolution_convert_fusion = bf16[768,1536]{1,0:T(8,128)(2,1)} fusion(bf16[768,768]{0,1:T(8,128)(2,1)} %bitcast.56, bf16[768,1536]{1,0:T(8,128)(2,1)} %copy-done.2), kind=kOutput, calls=%fused_computation | convolution fusion | flops 1813118976 | bytes 5898240 | tf_op jit(solution)/shard_map/dot_general | solution.py:139
  142.1 6.1 %all-to-all-done.3 = bf16[8,24,768]{2,1,0:T(8,128)(2,1)S(1)} async-done(((bf16[8,24,768]{2,1,0:T(8,128)(2,1)}), bf16[8,24,768]{2,1,0:T(8,128)(2,1)S(1)}, u32[]{:S(2)}, u32[]{:S(2)}) %all-to-all-start.3) | async-done | bytes 294944 | tf_op jit(solution)/shard_map/all_to_all | solution.py:32
  (50 shorter events, 12.9 us)
Async XLA Ops:
  0.6 37.9 %copy-start = (bf16[768,1536]{1,0:T(8,128)(2,1)S(1)}, bf16[768,1536]{1,0:T(8,128)(2,1)}, u32[]{:S(2)}) copy-start(bf16[768,1536]{1,0:T(8,128)(2,1)} %param.4) | copy-start | bytes 7077892
  39.6 4.7 %collective-permute-start = (bf16[4,96,1536]{2,1,0:T(8,128)(2,1)S(1)}, bf16[4,96,1536]{2,1,0:T(8,128)(2,1)S(1)}, u32[]{:S(2)}, u32[]{:S(2)}) collective-permute-start(bf16[4,96,1536]{2,1,0:T(8,128)(2,1)S(1)} %bitcast.61), channel_id=1, source_target_pairs={{0,1},{1,0},{2,3},{3,2},{4,5},{5,4},{6,7},{7,6},{8,9},{9,8},{10,11... | collective-permute-start | bytes 3538952 | tf_op jit(solution)/shard_map/ppermute | solution.py:44
  44.4 11.9 %collective-permute-start.3 = (bf16[96,768]{1,0:T(8,128)(2,1)S(1)}, bf16[96,768]{1,0:T(8,128)(2,1)S(1)}, u32[]{:S(2)}, u32[]{:S(2)}) collective-permute-start(bf16[96,768]{1,0:T(8,128)(2,1)S(1)} %fusion.14), channel_id=1, source_target_pairs={{0,4},{1,13},{2,6},{3,15},{4,8},{5,1},{6,10},{7,3},{8,12},{9,5},{1... | collective-permute-start | bytes 442376 | tf_op jit(solution)/shard_map/ppermute | solution.py:52
  49.6 9.8 %collective-permute-start.2 = (bf16[96,1536]{1,0:T(8,128)(2,1)S(1)}, bf16[96,1536]{1,0:T(8,128)(2,1)S(1)}, u32[]{:S(2)}, u32[]{:S(2)}) collective-permute-start(bf16[96,1536]{1,0:T(8,128)(2,1)S(1)} %get-tuple-element.22), channel_id=1, source_target_pairs={{0,2},{1,15},{2,4},{3,1},{4,6},{5,3},{6,8},{7,5},{8,10},{9,7},{10,... | collective-permute-start | bytes 884744 | tf_op jit(solution)/shard_map/ppermute | solution.py:52
  53.7 18.0 %collective-permute-start.1 = (bf16[96,1536]{1,0:T(8,128)(2,1)S(1)}, bf16[96,1536]{1,0:T(8,128)(2,1)S(1)}, u32[]{:S(2)}, u32[]{:S(2)}) collective-permute-start(bf16[96,1536]{1,0:T(8,128)(2,1)S(1)} %get-tuple-element.21), channel_id=1, source_target_pairs={{0,2},{1,15},{2,4},{3,1},{4,6},{5,3},{6,8},{7,5},{8,10},{9,7},{10,... | collective-permute-start | bytes 884744 | tf_op jit(solution)/shard_map/ppermute | solution.py:52
  59.6 13.7 %copy-start.1 = (bf16[48,1536]{1,0:T(8,128)(2,1)S(1)}, bf16[48,1536]{1,0:T(8,128)(2,1)}, u32[]{:S(2)}) copy-start(bf16[48,1536]{1,0:T(8,128)(2,1)} %param.5) | copy-start | bytes 442372
  59.6 13.1 %collective-permute-start.4 = (bf16[96,1536]{1,0:T(8,128)(2,1)S(1)}, bf16[96,1536]{1,0:T(8,128)(2,1)S(1)}, u32[]{:S(2)}, u32[]{:S(2)}) collective-permute-start(bf16[96,1536]{1,0:T(8,128)(2,1)S(1)} %fusion.11), channel_id=1, source_target_pairs={{0,4},{1,13},{2,6},{3,15},{4,8},{5,1},{6,10},{7,3},{8,12},{9,5},{1... | collective-permute-start | bytes 884744 | tf_op jit(solution)/shard_map/ppermute | solution.py:52
  73.3 3.7 %collective-permute-start.5 = (bf16[144,1536]{1,0:T(8,128)(2,1)S(1)}, bf16[144,1536]{1,0:T(8,128)(2,1)S(1)}, u32[]{:S(2)}, u32[]{:S(2)}) collective-permute-start(bf16[144,1536]{1,0:T(8,128)(2,1)S(1)} %pad_maximum_fusion.2), channel_id=1, source_target_pairs={{0,1},{1,0},{2,3},{3,2},{4,5},{5,4},{6,7},{7,6},{8,9},{9,8},{10,11... | collective-permute-start | bytes 1327112 | tf_op jit(solution)/shard_map/ppermute | solution.py:44
  77.6 12.8 %collective-permute-start.7 = (bf16[96,1536]{1,0:T(8,128)(2,1)S(1)}, bf16[96,1536]{1,0:T(8,128)(2,1)S(1)}, u32[]{:S(2)}, u32[]{:S(2)}) collective-permute-start(bf16[96,1536]{1,0:T(8,128)(2,1)S(1)} %get-tuple-element.20), channel_id=1, source_target_pairs={{0,4},{1,13},{2,6},{3,15},{4,8},{5,1},{6,10},{7,3},{8,12},{9,5},{1... | collective-permute-start | bytes 884744 | tf_op jit(solution)/shard_map/ppermute | solution.py:52
  80.9 14.4 %collective-permute-start.6 = (bf16[96,1536]{1,0:T(8,128)(2,1)S(1)}, bf16[96,1536]{1,0:T(8,128)(2,1)S(1)}, u32[]{:S(2)}, u32[]{:S(2)}) collective-permute-start(bf16[96,1536]{1,0:T(8,128)(2,1)S(1)} %get-tuple-element.20), channel_id=1, source_target_pairs={{0,2},{1,15},{2,4},{3,1},{4,6},{5,3},{6,8},{7,5},{8,10},{9,7},{10,... | collective-permute-start | bytes 884744 | tf_op jit(solution)/shard_map/ppermute | solution.py:52
  90.5 15.6 %collective-permute-start.9 = (bf16[96,1536]{1,0:T(8,128)(2,1)S(1)}, bf16[96,1536]{1,0:T(8,128)(2,1)S(1)}, u32[]{:S(2)}, u32[]{:S(2)}) collective-permute-start(bf16[96,1536]{1,0:T(8,128)(2,1)S(1)} %collective-permute-done.7), channel_id=1, source_target_pairs={{0,2},{1,15},{2,4},{3,1},{4,6},{5,3},{6,8},{7,5},{8,10},{9,7},{10,... | collective-permute-start | bytes 884744 | tf_op jit(solution)/shard_map/ppermute | solution.py:52
  95.4 10.6 %collective-permute-start.10 = (bf16[96,768]{1,0:T(8,128)(2,1)S(1)}, bf16[96,768]{1,0:T(8,128)(2,1)S(1)}, u32[]{:S(2)}, u32[]{:S(2)}) collective-permute-start(bf16[96,768]{1,0:T(8,128)(2,1)S(1)} %slice_select_fusion.2), channel_id=1, source_target_pairs={{0,4},{1,13},{2,6},{3,15},{4,8},{5,1},{6,10},{7,3},{8,12},{9,5},{1... | collective-permute-start | bytes 442376 | tf_op jit(solution)/shard_map/ppermute | solution.py:52
  97.3 10.7 %collective-permute-start.8 = (bf16[192,1536]{1,0:T(8,128)(2,1)S(1)}, bf16[192,1536]{1,0:T(8,128)(2,1)S(1)}, u32[]{:S(2)}, u32[]{:S(2)}) collective-permute-start(bf16[192,1536]{1,0:T(8,128)(2,1)S(1)} %pad_maximum_fusion.1), channel_id=1, source_target_pairs={{0,1},{1,0},{2,3},{3,2},{4,5},{5,4},{6,7},{7,6},{8,9},{9,8},{10,11... | collective-permute-start | bytes 1769480 | tf_op jit(solution)/shard_map/ppermute | solution.py:44
  106.0 3.7 %collective-permute-start.11 = (bf16[96,2304]{1,0:T(8,128)(2,1)S(1)}, bf16[96,2304]{1,0:T(8,128)(2,1)S(1)}, u32[]{:S(2)}, u32[]{:S(2)}) collective-permute-start(bf16[96,2304]{1,0:T(8,128)(2,1)S(1)} %pad_maximum_fusion.3), channel_id=1, source_target_pairs={{0,1},{1,0},{2,3},{3,2},{4,5},{5,4},{6,7},{7,6},{8,9},{9,8},{10,11... | collective-permute-start | bytes 1327112 | tf_op jit(solution)/shard_map/ppermute | solution.py:44
  109.9 2.0 %copy-start.2 = (bf16[768,1536]{1,0:T(8,128)(2,1)}, bf16[768,1536]{1,0:T(8,128)(2,1)S(1)}, u32[]{:S(2)}) copy-start(bf16[768,1536]{1,0:T(8,128)(2,1)S(1)} %constant_dynamic-update-slice_fusion) | copy-start | bytes 7077892
  132.3 15.9 %all-to-all-start.3 = ((bf16[8,24,768]{2,1,0:T(8,128)(2,1)}), bf16[8,24,768]{2,1,0:T(8,128)(2,1)S(1)}, u32[]{:S(2)}, u32[]{:S(2)}) async-start(bf16[8,24,768]{2,1,0:T(8,128)(2,1)} %reduce_sum.24), calls=%async_computation.3 | async-start | bytes 589824 | tf_op jit(solution)/shard_map/all_to_all | solution.py:32
